TPU v7x, 32 devices: a whole 2x2x4 slice. The times are simulated.
32 devices in a mesh: runs: 2 (over y), slab: 4 (over z), beads: 2 (over x), sub: 2 (over core).
Axes of the slice: x: 2, y: 2, z: 4, core: 2. Of those that a mesh axis runs over, the one named last changes fastest.
Arguments:
- dest_slab: int32 [131072, 1], P(('runs', 'slab', 'beads', 'sub')), parts along dimension 0, may hold values from 0 to 3; in each aligned block of 4096 rows (0 to 4095, 4096 to 8191, ...) at most 2048 rows name the same one
- local_cell: int32 [131072], P(('runs', 'slab', 'beads', 'sub')), parts along dimension 0, may hold values from 0 to 65535
- species: int32 [131072], P(('runs', 'slab', 'beads', 'sub')), parts along dimension 0, may hold values from 0 to 3
- bead_mass: float32 [131072], P(('runs', 'slab', 'beads', 'sub')), parts along dimension 0, may hold values from 0.5 to 1.5
- rise_fraction: float32 [131072], P(('runs', 'slab', 'beads', 'sub')), parts along dimension 0, may hold values from 0 to 1
- chi_matrix: float32 [4, 4], replicated, may hold values from 0 to 3
Outputs:
- potential: float32 [8, 8, 256, 128], P('runs', 'slab', ('beads', 'sub')), parts along dimension 0
- force: float32 [3, 8, 8, 256, 128], P(None, 'runs', 'slab', ('beads', 'sub')), parts along dimension 1
There are 2 independent parts, one for each index of `runs`. A program takes and returns all parts, laid end to end along the dimension named above; an argument that names none is the same for every part. Nothing has to cross between parts.
Inputs may be any that keep to these rules, and one draw needn't show every extreme that they name: `dest_slab`: among the 4096 beads of one device, no slab is named more than 2048 times, a bound that some block reaches.
All inputs are finite; a program needn't handle non-finite values.
Results may differ from a plain program's by a relative error of at most 0.0003.
Values sent between devices are 32-bit elements; how exact they have to be, the bound alone decides.
No kernel may reach another device: no remote copies, remote signals or barrier semaphores. Data moves between devices by JAX's collectives and lax.ppermute only.
A program may use at most 64 MiB of HBM per device.

v0:
```python
import jax
import jax.numpy as jnp
from jax import lax
from jax.sharding import PartitionSpec as P

S = 4
X = 256
Y = 128
CZ = 2


compress = 0.5


def passed_along(x, axis, by):
    length = lax.axis_size(axis)
    return lax.ppermute(x, axis, [(i, (i + by) % length) for i in range(length)])


def extended(block, sides, width):
    for axis, dim in sides:
        count = lax.axis_size(axis)
        forward = [(i, i + 1) for i in range(count - 1)]
        forward.append((count - 1, 0))
        backward = [(target, source) for source, target in forward]
        low = lax.ppermute(
            lax.slice_in_dim(block, block.shape[dim] - width, None, axis=dim), axis, forward
        )
        high = lax.ppermute(lax.slice_in_dim(block, 0, width, axis=dim), axis, backward)
        block = jnp.concatenate([low, block, high], axis=dim)
    return block


def smooth_padded(padded, along, length):

    def window(offset):
        return lax.slice_in_dim(padded, offset, offset + length, axis=along)

    return 0.375 * window(2) + 0.25 * (window(1) + window(3)) + 0.0625 * (window(0) + window(4))


def smooth_roll(values, along):
    near = jnp.roll(values, 1, along) + jnp.roll(values, -1, along)
    far = jnp.roll(values, 2, along) + jnp.roll(values, -2, along)
    return 0.375 * values + 0.25 * near + 0.0625 * far


def on_device(dest_slab, local_cell, species, bead_mass, rise_fraction, chi_matrix):
    bead_count = local_cell.shape[0]
    slab_count = lax.axis_size("slab")
    group_count = lax.axis_size(("beads", "sub"))
    plane_cells = X * Y
    lower_mass = bead_mass * (1.0 - rise_fraction)
    upper_mass = bead_mass * rise_fraction
    target = dest_slab[:, 0]
    capacity = 2 * bead_count // slab_count
    bead_order = jnp.argsort(target, stable=True)
    sorted_target = target[bead_order]
    buckets = jnp.arange(slab_count, dtype=jnp.int32)
    matches = sorted_target[:, None] == buckets[None, :]
    bucket_sizes = jnp.sum(matches, 0, dtype=jnp.int32)
    bucket_starts = jnp.cumsum(bucket_sizes) - bucket_sizes
    offsets = jnp.sum(jnp.where(matches, bucket_starts[None, :], 0), 1)
    within = jnp.arange(bead_count, dtype=jnp.int32) - offsets
    slot_index = sorted_target * capacity + within
    cell_index = species * ((CZ + 1) * plane_cells) + local_cell
    amounts = jnp.stack([lower_mass, upper_mass])[:, bead_order]
    send_amounts = jnp.zeros((2, slab_count * capacity), jnp.float32).at[:, slot_index].set(amounts)
    send_amounts = send_amounts.reshape(2, slab_count, capacity)
    send_index = (
        jnp.zeros((slab_count * capacity,), jnp.int32).at[slot_index].set(cell_index[bead_order])
    )
    send_index = send_index.reshape(1, slab_count, capacity)
    got_amounts, got_index = (
        lax.all_to_all(send_amounts, "slab", split_axis=1, concat_axis=1, tiled=True),
        lax.all_to_all(send_index, "slab", split_axis=1, concat_axis=1, tiled=True),
    )
    flat_index = got_index.reshape(-1)
    partial_value = jnp.zeros((S * (CZ + 1) * plane_cells,), jnp.float32)
    partial_value = partial_value.at[flat_index].add(got_amounts[0].reshape(-1))
    partial_value = partial_value.at[flat_index + plane_cells].add(got_amounts[1].reshape(-1))
    partial_value = partial_value.reshape(S, CZ + 1, X, Y)
    summed = lax.psum_scatter(partial_value, ("beads", "sub"), scatter_dimension=2, tiled=True)
    spilled = passed_along(summed[:, CZ:], "slab", 1)
    density = summed[:, :CZ].at[:, :1].add(spilled)
    piece_rows = X // group_count
    mean_density = bead_count * group_count / (CZ * X * Y)
    scaled = density / mean_density
    padded = extended(scaled, (("slab", 1), (("beads", "sub"), 2)), 2)
    smooth = smooth_padded(padded, 1, CZ)
    smooth = smooth_padded(smooth, 2, piece_rows)
    smooth = smooth_roll(smooth, 3)
    coupling = 0.5 * (chi_matrix + chi_matrix.T)
    potential = jnp.einsum("ab,bzxy->azxy", coupling, smooth, precision=lax.Precision.HIGHEST)
    potential = potential + (jnp.sum(smooth, 0) - 1.0) / compress
    rimmed = extended(potential, (("slab", 1), (("beads", "sub"), 2)), 1)
    force_height = -(rimmed[:, 2:, 1:-1] - rimmed[:, :-2, 1:-1]) * 0.5
    force_row = -(rimmed[:, 1:-1, 2:] - rimmed[:, 1:-1, :-2]) * 0.5
    force_lane = -(jnp.roll(potential, -1, 3) - jnp.roll(potential, 1, 3)) * 0.5
    force = jnp.stack([force_height, force_row, force_lane])
    return (potential, force)


def solution(mesh):
    placed = (
        P(("runs", "slab", "beads", "sub"), None),
        P(("runs", "slab", "beads", "sub")),
        P(("runs", "slab", "beads", "sub")),
        P(("runs", "slab", "beads", "sub")),
        P(("runs", "slab", "beads", "sub")),
        P(),
    )
    return jax.shard_map(
        on_device,
        mesh=mesh,
        in_specs=placed,
        out_specs=(
            P("runs", "slab", ("beads", "sub"), None),
            P(None, "runs", "slab", ("beads", "sub"), None),
        ),
        check_vma=False,
    )
```

profile of v0, /device:TPU:0, one launch (start us, length us, event | category | flops | bytes accessed | tf_op | source)
XLA Modules:
  0.0 313.8 jit_solution(1831599412186688261)
XLA Ops:
  7.2 6.5 %sort.17 = (s32[4096]{0:T(1024)}, s32[4096]{0:T(1024)S(1)}) sort(s32[4096]{0:T(1024)} %bitcast.39, s32[4096]{0:T(1024)S(1)} %iota.12), dimensions={0}, to_apply=%region_0.0 | sort | flops 49152 | bytes 65536 | tf_op jit(solution)/shard_map/jit(argsort)/sort | solution.py:57
  13.7 0.7 fusion.29
  14.5 23.0 %gather_fusion = s32[4096]{0:T(1024)S(1)} fusion(s32[4096]{0:T(1024)S(1)} %bitcast.40, s32[4096]{0:T(1024)S(1)} %get-tuple-element.52), kind=kCustom, calls=%fused_computation | custom fusion | bytes 49152 | tf_op jit(solution)/shard_map/gather | solution.py:58
  38.0 23.0 %gather_fusion.1 = s32[4096]{0:T(1024)S(1)} fusion(s32[4096]{0:T(1024)S(1)} %get-tuple-element.53, s32[4096]{0:T(1024)S(1)} %get-tuple-element.52), kind=kCustom, calls=%fused_computation.1 | custom fusion | bytes 49152 | tf_op jit(solution)/shard_map/gather | solution.py:71
  61.1 16.1 %scatter_custom_fusion = s32[8192]{0:T(1024)} fusion(s32[4096]{0:T(1024)S(1)} %bitcast.54, s32[4096]{0:T(1024)S(1)} %gather_fusion.1, s32[]{:T(128)} %constant.58.clone.1), kind=kCustom, calls=%fused_computation.75 | custom fusion | bytes 32772 | tf_op jit(solution)/shard_map/scatter | solution.py:71
  77.2 6.3 %all-to-all-start = ((s32[1,4,2048]{2,0,1:T(1,128)}), s32[1,4,2048]{2,0,1:T(1,128)S(1)}, u32[]{:S(2)}, u32[]{:S(2)}) async-start(s32[1,4,2048]{2,0,1:T(1,128)} %bitcast.9), calls=%async_computation | async-start | bytes 65536 | tf_op jit(solution)/shard_map/all_to_all | solution.py:76
  83.6 0.6 copy.35
  84.2 26.8 %scatter_custom_fusion.1 = f32[2,8192]{0,1:T(8,128)} fusion(s32[4096]{0:T(1024)S(1)} %bitcast.55, f32[2,4096]{0,1:T(8,128)S(1)} %copy.35, s32[4096]{0:T(1024)S(1)} %get-tuple-element.52, f32[]{:T(128)} %constant.57.clone.1), kind=kCustom, calls=%fused_computation.7 | custom fusion | bytes 65540 | tf_op jit(solution)/shard_map/scatter | solution.py:68
  111.0 3.5 %copy.36 = f32[2,4,2048]{2,0,1:T(2,128)} copy(f32[2,4,2048]{0,2,1:T(8,128)} %bitcast.42) | data formatting | bytes 131072 | tf_op jit(solution)/shard_map/reshape | solution.py:69
  114.5 5.1 %all-to-all-start.1 = ((f32[2,4,2048]{2,0,1:T(2,128)}), f32[2,4,2048]{2,0,1:T(2,128)S(1)}, u32[]{:S(2)}, u32[]{:S(2)}) async-start(f32[2,4,2048]{2,0,1:T(2,128)} %copy.36), calls=%async_computation.1 | async-start | bytes 131072 | tf_op jit(solution)/shard_map/all_to_all | solution.py:75
  119.7 5.7 %all-to-all-done.1 = f32[2,4,2048]{2,0,1:T(2,128)S(1)} async-done(((f32[2,4,2048]{2,0,1:T(2,128)}), f32[2,4,2048]{2,0,1:T(2,128)S(1)}, u32[]{:S(2)}, u32[]{:S(2)}) %all-to-all-start.1) | async-done | bytes 65568 | tf_op jit(solution)/shard_map/all_to_all | solution.py:75
  125.4 43.8 %scatter_custom_fusion.2 = f32[393216]{0:T(1024)S(1)} fusion(s32[8192]{0:T(1024)S(1)} %bitcast.50, f32[8192]{0:T(1024)S(1)} %bitcast.51, f32[]{:T(128)} %constant.57.clone.1), kind=kCustom, calls=%fused_computation.13 | custom fusion | flops 8192 | bytes 1572868 | tf_op jit(solution)/shard_map/scatter-add | solution.py:80
  169.2 45.0 %scatter_fusion = f32[393216]{0:T(1024)S(1)} fusion(f32[393216]{0:T(1024)S(1)} %scatter_custom_fusion.2, s32[8192]{0:T(1024)S(1)} %bitcast.43, f32[8192]{0:T(1024)S(1)} %bitcast.44), kind=kCustom, calls=%fused_computation.6 | custom fusion | flops 8192 | bytes 131072 | tf_op jit(solution)/shard_map/scatter-add | solution.py:81
  214.2 1.1 copy-done.1
  215.4 48.6 %reduce-scatter.2.cloned.1.call-done = f32[4,3,64,128]{3,2,1,0:T(8,128)} async-done(((f32[4,3,256,128]{3,2,1,0:T(8,128)}), f32[4,3,64,128]{3,2,1,0:T(8,128)}) %reduce-scatter.2.cloned.1.call-update) | async-done | bytes 393232 | tf_op jit(solution)/shard_map/reduce_scatter | solution.py:83
  264.0 0.9 slice.197
  264.9 1.5 collective-permute-start
  266.4 1.0 slice.195
  267.4 4.6 %collective-permute-done = f32[4,1,64,128]{3,2,1,0:T(8,128)S(1)} collective-permute-done((f32[4,1,64,128]{3,2,1,0:T(8,128)S(1)}, f32[4,1,64,128]{3,2,1,0:T(8,128)S(1)}, u32[]{:S(2)}, u32[]{:S(2)}) %collective-permute-start) | collective-permute-done | bytes 131104 | tf_op jit(solution)/shard_map/ppermute | solution.py:17
  272.0 0.9 fusion.28
  273.0 3.8 %collective-permute-start.2 = (f32[4,2,64,128]{3,2,1,0:T(8,128)S(1)}, f32[4,2,64,128]{3,2,1,0:T(8,128)S(1)}, u32[]{:S(2)}, u32[]{:S(2)}) collective-permute-start(f32[4,2,64,128]{3,2,1,0:T(8,128)S(1)} %broadcast_multiply_fusion), channel_id=1, source_target_pairs={{4,0},{8,4},{12,8},{0,12},{5,1},{9,5},{13,9},{1,13},{6,2},{10,6},{... | collective-permute-start | bytes 786440 | tf_op jit(solution)/shard_map/ppermute | solution.py:29
  276.8 7.2 %collective-permute-done.1 = f32[4,2,64,128]{3,2,1,0:T(8,128)S(1)} collective-permute-done((f32[4,2,64,128]{3,2,1,0:T(8,128)S(1)}, f32[4,2,64,128]{3,2,1,0:T(8,128)S(1)}, u32[]{:S(2)}, u32[]{:S(2)}) %collective-permute-start.1) | collective-permute-done | bytes 262176 | tf_op jit(solution)/shard_map/ppermute | solution.py:26
  284.0 1.8 collective-permute-done.2
  285.9 1.7 collective-permute-start.4
  287.7 1.4 collective-permute-done.3
  290.5 0.7 convolution_add_fusion
  291.4 2.1 collective-permute-start.5
  294.4 3.3 %collective-permute-done.5 = f32[4,1,64,128]{3,0,2,1:T(4,128)S(1)} collective-permute-done((f32[4,1,64,128]{3,0,2,1:T(4,128)S(1)}, f32[4,1,64,128]{3,0,2,1:T(4,128)S(1)}, u32[]{:S(2)}, u32[]{:S(2)}) %collective-permute-start.5) | collective-permute-done | bytes 131104 | tf_op jit(solution)/shard_map/ppermute | solution.py:29
  297.6 4.6 %collective-permute-done.6 = f32[4,1,64,128]{3,0,2,1:T(4,128)S(1)} collective-permute-done((f32[4,1,64,128]{3,0,2,1:T(4,128)S(1)}, f32[4,1,64,128]{3,0,2,1:T(4,128)S(1)}, u32[]{:S(2)}, u32[]{:S(2)}) %collective-permute-start.6) | collective-permute-done | bytes 131104 | tf_op jit(solution)/shard_map/ppermute | solution.py:26
  303.1 0.7 copy.42
  303.9 1.7 collective-permute-done.8
  305.9 1.0 copy.43
  (53 shorter events, 4.5 us)
Async XLA Ops:
  7.2 7.3 %copy-start = (s32[4096,1]{0,1:T(1,128)S(1)}, s32[4096,1]{0,1:T(1,128)}, u32[]{:S(2)}) copy-start(s32[4096,1]{0,1:T(1,128)} %param.8) | copy-start | bytes 49156
  38.0 45.5 %copy-start.2 = (f32[4096]{0:T(1024)S(1)}, f32[4096]{0:T(1024)}, u32[]{:S(2)}) copy-start(f32[4096]{0:T(1024)} %param.11) | copy-start | bytes 49156
  38.0 45.5 %copy-start.3 = (f32[4096]{0:T(1024)S(1)}, f32[4096]{0:T(1024)}, u32[]{:S(2)}) copy-start(f32[4096]{0:T(1024)} %param.12) | copy-start | bytes 49156
  77.2 37.3 %all-to-all-start = ((s32[1,4,2048]{2,0,1:T(1,128)}), s32[1,4,2048]{2,0,1:T(1,128)S(1)}, u32[]{:S(2)}, u32[]{:S(2)}) async-start(s32[1,4,2048]{2,0,1:T(1,128)} %bitcast.9), calls=%async_computation | async-start | bytes 65536 | tf_op jit(solution)/shard_map/all_to_all | solution.py:76
  114.5 10.8 %all-to-all-start.1 = ((f32[2,4,2048]{2,0,1:T(2,128)}), f32[2,4,2048]{2,0,1:T(2,128)S(1)}, u32[]{:S(2)}, u32[]{:S(2)}) async-start(f32[2,4,2048]{2,0,1:T(2,128)} %copy.36), calls=%async_computation.1 | async-start | bytes 131072 | tf_op jit(solution)/shard_map/all_to_all | solution.py:75
  119.6 144.4 %reduce-scatter.2.cloned.1.call-start = ((), (), s32[]{:S(2)}) async-start(), calls=%async_computation.3 | async-start | bytes 1966080 | tf_op jit(solution)/shard_map/reduce_scatter | solution.py:83
  214.2 1.2 copy-start.1
  214.2 73.5 %copy-start.4 = (f32[4,4]{1,0:T(4,128)S(1)}, f32[4,4]{1,0:T(4,128)}, u32[]{:S(2)}) copy-start(f32[4,4]{1,0:T(4,128)} %param.13) | copy-start | bytes 196
  264.9 7.1 %collective-permute-start = (f32[4,1,64,128]{3,2,1,0:T(8,128)S(1)}, f32[4,1,64,128]{3,2,1,0:T(8,128)S(1)}, u32[]{:S(2)}, u32[]{:S(2)}) collective-permute-start(f32[4,1,64,128]{3,2,1,0:T(8,128)S(1)} %slice.197), channel_id=1, source_target_pairs={{0,4},{4,8},{8,12},{12,0},{1,5},{5,9},{9,13},{13,1},{2,6},{6,10},{... | collective-permute-start | bytes 393224 | tf_op jit(solution)/shard_map/ppermute | solution.py:17
  272.9 11.1 %collective-permute-start.1 = (f32[4,2,64,128]{3,2,1,0:T(8,128)S(1)}, f32[4,2,64,128]{3,2,1,0:T(8,128)S(1)}, u32[]{:S(2)}, u32[]{:S(2)}) collective-permute-start(f32[4,2,64,128]{3,2,1,0:T(8,128)S(1)} %broadcast_multiply_fusion), channel_id=1, source_target_pairs={{0,4},{4,8},{8,12},{12,0},{1,5},{5,9},{9,13},{13,1},{2,6},{6,10},{... | collective-permute-start | bytes 786440 | tf_op jit(solution)/shard_map/ppermute | solution.py:26
  273.0 12.8 %collective-permute-start.2 = (f32[4,2,64,128]{3,2,1,0:T(8,128)S(1)}, f32[4,2,64,128]{3,2,1,0:T(8,128)S(1)}, u32[]{:S(2)}, u32[]{:S(2)}) collective-permute-start(f32[4,2,64,128]{3,2,1,0:T(8,128)S(1)} %broadcast_multiply_fusion), channel_id=1, source_target_pairs={{4,0},{8,4},{12,8},{0,12},{5,1},{9,5},{13,9},{1,13},{6,2},{10,6},{... | collective-permute-start | bytes 786440 | tf_op jit(solution)/shard_map/ppermute | solution.py:29
  285.9 3.3 %collective-permute-start.3 = (f32[4,6,2,128]{3,2,1,0:T(2,128)S(1)}, f32[4,6,2,128]{3,2,1,0:T(2,128)S(1)}, u32[]{:S(2)}, u32[]{:S(2)}) collective-permute-start(f32[4,6,2,128]{3,2,1,0:T(2,128)S(1)} %get-tuple-element.26), channel_id=1, source_target_pairs={{0,1},{1,2},{2,3},{3,0},{4,5},{5,6},{6,7},{7,4},{8,9},{9,10},{10,1... | collective-permute-start | bytes 73736 | tf_op jit(solution)/shard_map/ppermute | solution.py:26
  285.9 3.3 %collective-permute-start.4 = (f32[4,6,2,128]{3,2,1,0:T(2,128)S(1)}, f32[4,6,2,128]{3,2,1,0:T(2,128)S(1)}, u32[]{:S(2)}, u32[]{:S(2)}) collective-permute-start(f32[4,6,2,128]{3,2,1,0:T(2,128)S(1)} %get-tuple-element.27), channel_id=1, source_target_pairs={{1,0},{2,1},{3,2},{0,3},{5,4},{6,5},{7,6},{4,7},{9,8},{10,9},{11,1... | collective-permute-start | bytes 73736 | tf_op jit(solution)/shard_map/ppermute | solution.py:29
  291.4 6.2 %collective-permute-start.5 = (f32[4,1,64,128]{3,0,2,1:T(4,128)S(1)}, f32[4,1,64,128]{3,0,2,1:T(4,128)S(1)}, u32[]{:S(2)}, u32[]{:S(2)}) collective-permute-start(f32[4,1,64,128]{3,0,2,1:T(4,128)S(1)} %get-tuple-element.33), channel_id=1, source_target_pairs={{4,0},{8,4},{12,8},{0,12},{5,1},{9,5},{13,9},{1,13},{6,2},{10,6},{... | collective-permute-start | bytes 393224 | tf_op jit(solution)/shard_map/ppermute | solution.py:29
  293.5 8.8 %collective-permute-start.6 = (f32[4,1,64,128]{3,0,2,1:T(4,128)S(1)}, f32[4,1,64,128]{3,0,2,1:T(4,128)S(1)}, u32[]{:S(2)}, u32[]{:S(2)}) collective-permute-start(f32[4,1,64,128]{3,0,2,1:T(4,128)S(1)} %get-tuple-element.32), channel_id=1, source_target_pairs={{0,4},{4,8},{8,12},{12,0},{1,5},{5,9},{9,13},{13,1},{2,6},{6,10},{... | collective-permute-start | bytes 393224 | tf_op jit(solution)/shard_map/ppermute | solution.py:26
  302.2 1.7 collective-permute-start.7
  302.5 3.1 collective-permute-start.8
Sparse Core Ops, SparseCore 0:
  215.5 48.4 reduce-scatter.1
where the time goes:
time: 314 us
  local copies, waits for them, and re-layouts  99.6 us (32%)
  other arithmetic  99 us (32%)
  waiting for transfers between devices  79 us (25%)
  starting transfers between devices  21.2 us (7%)
  between operations  14.3 us (5%)
    reduce_scatter x1, waiting for transfers between devices, on_device(): lax.psum_scatter(partial_value, ('beads', 'sub'), scatter_dimension=2, ti...  48.6 us
    scatter-add x1, other arithmetic, on_device(): partial_value.at[flat_index + plane_cells].add(got_amounts[1].reshape(-1))  45 us
    scatter-add x1, other arithmetic, on_device(): partial_value = partial_value.at[flat_index].add(got_amounts[0].reshape(-1))  43.8 us
    scatter x1, local copies, waits for them, and re-layouts, on_device(): jnp.zeros((2, slab_count * capacity), jnp.float32).at[:, slot_index]  26.8 us
    gather x1, local copies, waits for them, and re-layouts, on_device(): sorted_target = target[bead_order]  23 us
    gather x1, local copies, waits for them, and re-layouts, on_device(): cell_index[bead_order]  23 us
    scatter x1, local copies, waits for them, and re-layouts, on_device(): jnp.zeros((slab_count * capacity,), jnp.int32).at[slot_index]  16.1 us
    ppermute x4, waiting for transfers between devices, extended(): lax.ppermute(lax.slice_in_dim(block, block.shape[dim] - width, None, axis...  14.9 us
  transfers between devices with their start and end apart: 12, of which 10 were waited for; matrix products, arithmetic and copies ran while one was open for 11% of the time, Pallas kernels for 0%

commit v1 on v0

v1 whole, which is shorter than its diff:
```python
import functools

import jax
import jax.numpy as jnp
from jax import lax
from jax.experimental import pallas as pl
from jax.experimental.pallas import tpu as pltpu
from jax.sharding import PartitionSpec as P

S = 4
X = 256
Y = 128
CZ = 2

compress = 0.5

BUCKET = 8
BUCKETS = X // BUCKET
RIM = 4
CHUNK = 256
BLOCK_LISTS = 16
TOGETHER = 4
WINDOW_BUCKETS = 3
WINDOW = WINDOW_BUCKETS * BUCKET

NT = (((1,), (1,)), ((), ()))


def pieces_of(values):
    parts = []
    for _ in range(2):
        part = values.astype(jnp.bfloat16)
        parts.append(part)
        values = values - part.astype(jnp.float32)
    parts.append(values.astype(jnp.bfloat16))
    return parts


def sort_kernel(heights, scale, dest_ref, cell_ref, species_ref, mass_ref, rise_ref, out_ref, left_ref, right_ref):
    lines = cell_ref.shape[0]
    places = lines * 128
    chunks = places // CHUNK
    cell = cell_ref[...]
    row = (cell // Y) % X
    height = dest_ref[...] * CZ + cell // (X * Y)
    key = (species_ref[...] * heights + height) * (X * Y) + cell % (X * Y)
    mass = mass_ref[...] * scale
    lower = mass * (1.0 - rise_ref[...])
    upper = mass * rise_ref[...]
    bucket = ((row + RIM) % X) // BUCKET
    member_iota = lax.broadcasted_iota(jnp.int32, (BUCKETS, 128), 0)
    members = [
        jnp.where(bucket[i : i + 1, :] == member_iota, 1.0, 0.0) for i in range(lines)
    ]
    stacked = jnp.concatenate([m.astype(jnp.bfloat16) for m in members], 0)
    source = lax.broadcasted_iota(jnp.int32, (128, 256), 0)
    target = lax.broadcasted_iota(jnp.int32, (128, 256), 1)
    before = jnp.where(source < target, 1.0, 0.0).astype(jnp.bfloat16)
    counted = jnp.dot(stacked, before, preferred_element_type=jnp.float32)
    total = jnp.zeros((BUCKETS, 128), jnp.float32)
    ranks = []
    for i in range(lines):
        ranks.append(counted[i * BUCKETS : (i + 1) * BUCKETS, :128] + total)
        total = total + counted[i * BUCKETS : (i + 1) * BUCKETS, 128:]
    start = total
    shift = 1
    while shift < BUCKETS:
        start = start + jnp.where(member_iota >= shift, pltpu.roll(start, shift, 0), 0.0)
        shift *= 2
    start = start - total
    lane = lax.broadcasted_iota(jnp.int32, (BUCKETS, 128), 1)
    starts = jnp.sum(jnp.where(member_iota == lane, start, 0.0), 0, keepdims=True)
    starts = jnp.where(lane[:1] < BUCKETS, starts, float(places))
    key_parts = [
        part.astype(jnp.float32).astype(jnp.bfloat16) for part in (key // 65536, (key // 256) % 256, key % 256)
    ]
    parts = key_parts + pieces_of(lower) + pieces_of(upper)
    parts = [part.astype(jnp.float32) for part in parts]
    chunk_iota = lax.broadcasted_iota(jnp.int32, (chunks, 128), 0)
    slot_iota = lax.broadcasted_iota(jnp.int32, (CHUNK, 128), 0)
    for i in range(lines):
        place = jnp.sum(members[i] * (ranks[i] + start), 0, keepdims=True).astype(jnp.int32)
        hit = chunk_iota == place // CHUNK
        for n, part in enumerate(parts):
            left_ref[n * chunks : (n + 1) * chunks, i * 128 : (i + 1) * 128] = jnp.where(
                hit, part[i : i + 1, :], 0.0
            ).astype(jnp.bfloat16)
        right_ref[:, i * 128 : (i + 1) * 128] = jnp.where(
            slot_iota == place % CHUNK, 1.0, 0.0
        ).astype(jnp.bfloat16)
    placed = lax.dot_general(
        left_ref[...], right_ref[...], NT, preferred_element_type=jnp.float32
    )

    def part_of(n):
        return placed[n * chunks : (n + 1) * chunks]

    out_ref[0:chunks] = part_of(0) * 65536.0 + part_of(1) * 256.0 + part_of(2)
    out_ref[chunks : 2 * chunks] = part_of(3) + part_of(4) + part_of(5)
    out_ref[2 * chunks : 3 * chunks] = part_of(6) + part_of(7) + part_of(8)
    out_ref[3 * chunks : 3 * chunks + 8] = jnp.broadcast_to(
        jnp.concatenate([starts, starts], 1), (8, CHUNK)
    )


def grid_kernel(
    heights,
    own_rows,
    chi_ref,
    place_ref,
    lists_ref,
    potential_ref,
    force_ref,
    near_ref,
    column_ref,
    amount_ref,
    starts_ref,
    starts_smem,
    grid_ref,
    sem,
):
    lists = lists_ref.shape[0]
    chunks = (lists_ref.shape[1] - 8) // 3
    places = chunks * CHUNK
    windows = -(-(own_rows // BUCKET + 1) // WINDOW_BUCKETS)
    slab = place_ref[0]
    group = place_ref[1]
    step = pl.program_id(0)

    starts_ref[...] = lists_ref[:, 3 * chunks, :128].astype(jnp.int32)
    copy = pltpu.make_async_copy(starts_ref, starts_smem, sem)
    copy.start()

    @pl.when(step == 0)
    def _():
        grid_ref[...] = jnp.zeros_like(grid_ref)

    first_row = group * own_rows - RIM

    def spread(i, carry):
        key = lists_ref[i, 0:chunks, :].astype(jnp.int32)
        lower = lists_ref[i, chunks : 2 * chunks, :]
        upper = lists_ref[i, 2 * chunks : 3 * chunks, :]
        spot = pl.ds(pl.multiple_of(i * chunks, chunks), chunks)
        species = key // (heights * X * Y)
        height = (key // (X * Y)) % heights
        row = (key // Y) % X
        near_ref[spot, :] = (row - first_row + X) % X + (species // 2) * 1024
        column_ref[spot, :] = key % Y + (species % 2) * Y
        shares = (
            0.0625 * lower,
            0.25 * lower + 0.0625 * upper,
            0.375 * lower + 0.25 * upper,
            0.25 * lower + 0.375 * upper,
            0.0625 * lower + 0.25 * upper,
            0.0625 * upper,
        )
        for n in range(CZ + 2):
            above = (slab * CZ - 1 + n + 2 + heights - height) % heights
            amount = jnp.zeros_like(lower)
            for d, share in enumerate(shares):
                amount = jnp.where(above == d, share, amount)
            high = amount.astype(jnp.bfloat16).astype(jnp.float32)
            amount_ref[2 * n, spot, :] = high
            amount_ref[2 * n + 1, spot, :] = amount - high
        return carry

    lax.fori_loop(0, lists, spread, 0)
    copy.wait()

    near_iota = lax.broadcasted_iota(jnp.int32, (2 * WINDOW, CHUNK), 0)
    near_iota = jnp.where(near_iota >= WINDOW, near_iota + (1024 - WINDOW), near_iota)
    column_iota = lax.broadcasted_iota(jnp.int32, (2 * Y, CHUNK), 0)

    def window_body(window, carry):
        def some_lists(some, carry):
            firsts, counts = [], []
            for u in range(TOGETHER):
                i = some * TOGETHER + u
                low = group * (own_rows // BUCKET) + window * WINDOW_BUCKETS
                high = low + WINDOW_BUCKETS
                wrapped = jnp.where(high > BUCKETS, BUCKETS, 0)
                begin = starts_smem[i, low]
                end = starts_smem[i, high - wrapped] + jnp.where(high > BUCKETS, places, 0)
                first = begin // CHUNK
                count = jnp.where(end > begin, (end + CHUNK - 1) // CHUNK - first, 0)
                firsts.append(first)
                counts.append(jnp.minimum(count, chunks))
            longest = functools.reduce(jnp.maximum, counts)

            def one_round(turn, carry):
                lefts, rights = [], []
                for u in range(TOGETHER):
                    line = (some * TOGETHER + u) * chunks + (firsts[u] + turn) % chunks
                    at = pl.ds(line, 1)
                    base = jnp.where(turn < counts[u], window * WINDOW, 8192)
                    hit = jnp.where(near_ref[at, :] - base == near_iota, 1.0, 0.0)
                    hit = hit.astype(jnp.bfloat16)
                    lefts.append(
                        jnp.concatenate(
                            [
                                hit * jnp.broadcast_to(amount_ref[n, at, :], hit.shape).astype(jnp.bfloat16)
                                for n in range(2 * (CZ + 2))
                            ],
                            0,
                        )
                    )
                    rights.append(
                        jnp.where(column_ref[at, :] == column_iota, 1.0, 0.0).astype(jnp.bfloat16)
                    )
                got = lax.dot_general(
                    jnp.concatenate(lefts, 1),
                    jnp.concatenate(rights, 1),
                    NT,
                    preferred_element_type=jnp.float32,
                )
                for n in range(CZ + 2):
                    for half in range(2):
                        at_high = (2 * n * 2 + half) * WINDOW
                        at_low = ((2 * n + 1) * 2 + half) * WINDOW
                        where = pl.ds(pl.multiple_of(window * WINDOW, BUCKET), WINDOW)
                        grid_ref[n, half, where, :] += (
                            got[at_high : at_high + WINDOW] + got[at_low : at_low + WINDOW]
                        )
                return carry

            return lax.fori_loop(0, longest, one_round, carry)

        return lax.fori_loop(0, lists // TOGETHER, some_lists, carry)

    lax.fori_loop(0, windows, window_body, 0)

    @pl.when(step == pl.num_programs(0) - 1)
    def _():
        rows = own_rows + 2

        def smooth_of(n, b):
            lanes = slice((b % 2) * Y, (b % 2 + 1) * Y)

            def shifted(k):
                return grid_ref[n, b // 2, RIM - 3 + k : RIM - 3 + k + rows, lanes]

            value = (
                0.375 * shifted(2) + 0.25 * (shifted(1) + shifted(3)) + 0.0625 * (shifted(0) + shifted(4))
            )
            close = pltpu.roll(value, 1, 1) + pltpu.roll(value, Y - 1, 1)
            far = pltpu.roll(value, 2, 1) + pltpu.roll(value, Y - 2, 1)
            return 0.375 * value + 0.25 * close + 0.0625 * far

        layers = []
        for n in range(CZ + 2):
            smooth = [smooth_of(n, b) for b in range(S)]
            layer = []
            for a in range(S):
                value = -1.0 / compress
                for b in range(S):
                    factor = 0.5 * (chi_ref[a, b] + chi_ref[b, a]) + 1.0 / compress
                    value = value + factor * smooth[b]
                layer.append(value)
            layers.append(layer)
        for a in range(S):
            for z in range(CZ):
                value = layers[z + 1][a]
                own = value[1:-1]
                potential_ref[a, z] = own
                force_ref[0, a, z] = (layers[z][a][1:-1] - layers[z + 2][a][1:-1]) * 0.5
                force_ref[1, a, z] = (value[:-2] - value[2:]) * 0.5
                force_ref[2, a, z] = (pltpu.roll(own, 1, 1) - pltpu.roll(own, Y - 1, 1)) * 0.5


def gathered(block):
    slab_count = lax.axis_size("slab")
    if slab_count > 8:
        block = lax.all_gather(block, "slab")
    else:
        turned = [
            lax.ppermute(block, "slab", [(i, (i + k) % slab_count) for i in range(slab_count)])
            for k in range(1, slab_count)
        ]
        block = jnp.stack([block] + turned)
    for axis in ("beads", "sub"):
        count = lax.axis_size(axis)
        turned = [
            lax.ppermute(block, axis, [(i, (i + k) % count) for i in range(count)])
            for k in range(1, count)
        ]
        block = jnp.concatenate([block] + turned)
    return block


def on_device(dest_slab, local_cell, species, bead_mass, rise_fraction, chi_matrix):
    bead_count = local_cell.shape[0]
    slab_count = lax.axis_size("slab")
    group_count = lax.axis_size(("beads", "sub"))
    heights = slab_count * CZ
    own_rows = X // group_count
    scale = CZ * X * Y / (bead_count * group_count)
    lines = bead_count // 128
    chunks = bead_count // CHUNK
    vmem = pl.BlockSpec(memory_space=pltpu.VMEM)
    smem = pl.BlockSpec(memory_space=pltpu.SMEM)
    block = pl.pallas_call(
        functools.partial(sort_kernel, heights, scale),
        out_shape=jax.ShapeDtypeStruct((3 * chunks + 8, CHUNK), jnp.float32),
        in_specs=[vmem] * 5,
        out_specs=vmem,
        scratch_shapes=[
            pltpu.VMEM((9 * chunks, bead_count), jnp.bfloat16),
            pltpu.VMEM((CHUNK, bead_count), jnp.bfloat16),
        ],
        compiler_params=pltpu.CompilerParams(vmem_limit_bytes=32 << 20),
        name="sort_beads",
    )(*[x.reshape(lines, 128) for x in (dest_slab, local_cell, species, bead_mass, rise_fraction)])
    lists = gathered(block)
    place = jnp.stack([lax.axis_index("slab"), lax.axis_index(("beads", "sub"))]).astype(jnp.int32)
    list_lines = 3 * chunks + 8
    windows = -(-(own_rows // BUCKET + 1) // WINDOW_BUCKETS)
    potential, force = pl.pallas_call(
        functools.partial(grid_kernel, heights, own_rows),
        grid=(lists.shape[0] // BLOCK_LISTS,),
        out_shape=(
            jax.ShapeDtypeStruct((S, CZ, own_rows, Y), jnp.float32),
            jax.ShapeDtypeStruct((3, S, CZ, own_rows, Y), jnp.float32),
        ),
        in_specs=[
            smem,
            smem,
            pl.BlockSpec((BLOCK_LISTS, list_lines, CHUNK), lambda i: (i, 0, 0)),
        ],
        out_specs=(
            pl.BlockSpec((S, CZ, own_rows, Y), lambda i: (0, 0, 0, 0)),
            pl.BlockSpec((3, S, CZ, own_rows, Y), lambda i: (0, 0, 0, 0, 0)),
        ),
        scratch_shapes=[
            pltpu.VMEM((BLOCK_LISTS * chunks, CHUNK), jnp.int32),
            pltpu.VMEM((BLOCK_LISTS * chunks, CHUNK), jnp.int32),
            pltpu.VMEM((2 * (CZ + 2), BLOCK_LISTS * chunks, CHUNK), jnp.float32),
            pltpu.VMEM((BLOCK_LISTS, 128), jnp.int32),
            pltpu.SMEM((BLOCK_LISTS, 128), jnp.int32),
            pltpu.VMEM((CZ + 2, 2, max(windows * WINDOW, own_rows + 2 * RIM), 2 * Y), jnp.float32),
            pltpu.SemaphoreType.DMA,
        ],
        compiler_params=pltpu.CompilerParams(vmem_limit_bytes=48 << 20),
        name="grid_fields",
    )(chi_matrix, place, lists)
    return (potential, force)


def solution(mesh):
    placed = (
        P(("runs", "slab", "beads", "sub"), None),
        P(("runs", "slab", "beads", "sub")),
        P(("runs", "slab", "beads", "sub")),
        P(("runs", "slab", "beads", "sub")),
        P(("runs", "slab", "beads", "sub")),
        P(),
    )
    return jax.shard_map(
        on_device,
        mesh=mesh,
        in_specs=placed,
        out_specs=(
            P("runs", "slab", ("beads", "sub"), None),
            P(None, "runs", "slab", ("beads", "sub"), None),
        ),
        check_vma=False,
    )
```

time: 314 us -> 45.8 us (0.15)
  the two profiles are of different devices: /device:TPU:0 before, /device:TPU:1 now
where the time goes in v1:
time: 45.8 us; the launch traced here: 45.4 us
  Pallas kernels  22.3 us (49%)
  starting transfers between devices  9.14 us (20%)
  waiting for transfers between devices  8.87 us (19%)
  local copies, waits for them, and re-layouts  4.33 us (9%)
  between operations  0.68 us (1%)
    pallas_call x1, Pallas kernels, on_device(): pl.pallas_call(functools.partial(grid_kernel, heights, own_rows), grid=(l...  20.2 us
    ppermute x2, waiting for transfers between devices, gathered(): lax.ppermute(block, axis, [(i, (i + k) % count) for i in range(count)])  5.87 us
    ppermute x3, starting transfers between devices, gathered(): lax.ppermute(block, 'slab', [(i, (i + k) % slab_count) for i in range(sla...  5.54 us
    unnamed x16, local copies, waits for them, and re-layouts  4.26 us
    ppermute x2, starting transfers between devices, gathered(): lax.ppermute(block, axis, [(i, (i + k) % count) for i in range(count)])  3.6 us
    ppermute x3, waiting for transfers between devices, gathered(): lax.ppermute(block, 'slab', [(i, (i + k) % slab_count) for i in range(sla...  3.01 us
    pallas_call x1, Pallas kernels, on_device(): pl.pallas_call(functools.partial(sort_kernel, heights, scale), out_shape=...  2.09 us
  transfers between devices with their start and end apart: 5, of which 5 were waited for; matrix products, arithmetic and copies ran while one was open for 0% of the time, Pallas kernels for 0%

profile of v1, /device:TPU:1, one launch (start us, length us, event | category | flops | bytes accessed | tf_op | source)
XLA Modules:
  0.0 45.4 jit_solution(16656292493752345328)
XLA Ops:
  0.6 0.0 copy-start
  0.6 0.7 %copy-done = s32[4096,1]{0,1:T(1,128)S(1)} copy-done((s32[4096,1]{0,1:T(1,128)S(1)}, s32[4096,1]{0,1:T(1,128)}, u32[]{:S(2)}) %copy-start) | copy-done | bytes 16408
  1.3 0.0 copy-start.1
  1.4 0.7 %copy-done.1 = s32[4096]{0:T(1024)S(1)} copy-done((s32[4096]{0:T(1024)S(1)}, s32[4096]{0:T(1024)}, u32[]{:S(2)}) %copy-start.1) | copy-done | bytes 16408
  2.1 0.0 copy-start.2
  2.1 0.7 %copy-done.2 = s32[4096]{0:T(1024)S(1)} copy-done((s32[4096]{0:T(1024)S(1)}, s32[4096]{0:T(1024)}, u32[]{:S(2)}) %copy-start.2) | copy-done | bytes 16408
  2.8 0.0 copy-start.3
  2.8 0.7 %copy-done.3 = f32[4096]{0:T(1024)S(1)} copy-done((f32[4096]{0:T(1024)S(1)}, f32[4096]{0:T(1024)}, u32[]{:S(2)}) %copy-start.3) | copy-done | bytes 16408
  3.5 0.0 copy-start.4
  3.5 0.7 %copy-done.4 = f32[4096]{0:T(1024)S(1)} copy-done((f32[4096]{0:T(1024)S(1)}, f32[4096]{0:T(1024)}, u32[]{:S(2)}) %copy-start.4) | copy-done | bytes 16408
  4.2 2.1 %sort_beads.1 = f32[56,256]{1,0:T(8,128)S(1)} custom-call(s32[32,128]{1,0:T(8,128)S(1)} %bitcast.20, s32[32,128]{1,0:T(8,128)S(1)} %bitcast.21, s32[32,128]{1,0:T(8,128)S(1)} %bitcast.22, f32[32,128]{1,0:T(8,128)S(1)} %bitcast.23, f32[32,128]{1,0:T(8,128)S(1)} %bitcast.24), custom_call_target="tpu_custom_call" | custom-call | tf_op jit(solution)/shard_map/sort_beads/pallas_call | solution.py:302
  6.3 2.2 %collective-permute-start = (f32[56,256]{1,0:T(8,128)S(1)}, f32[56,256]{1,0:T(8,128)S(1)}, u32[]{:S(2)}, u32[]{:S(2)}) collective-permute-start(f32[56,256]{1,0:T(8,128)S(1)} %sort_beads.1), channel_id=1, source_target_pairs={{0,4},{4,8},{8,12},{12,0},{1,5},{5,9},{9,13},{13,1},{2,6},{6,10},{... | collective-permute-start | bytes 172040 | tf_op jit(solution)/shard_map/ppermute | solution.py:277
  8.5 2.3 %collective-permute-start.1 = (f32[56,256]{1,0:T(8,128)S(1)}, f32[56,256]{1,0:T(8,128)S(1)}, u32[]{:S(2)}, u32[]{:S(2)}) collective-permute-start(f32[56,256]{1,0:T(8,128)S(1)} %sort_beads.1), channel_id=1, source_target_pairs={{0,8},{4,12},{8,0},{12,4},{1,9},{5,13},{9,1},{13,5},{2,10},{6,14},... | collective-permute-start | bytes 172040 | tf_op jit(solution)/shard_map/ppermute | solution.py:277
  10.8 1.1 %collective-permute-start.2 = (f32[56,256]{1,0:T(8,128)S(1)}, f32[56,256]{1,0:T(8,128)S(1)}, u32[]{:S(2)}, u32[]{:S(2)}) collective-permute-start(f32[56,256]{1,0:T(8,128)S(1)} %sort_beads.1), channel_id=1, source_target_pairs={{0,12},{4,0},{8,4},{12,8},{1,13},{5,1},{9,5},{13,9},{2,14},{6,2},{... | collective-permute-start | bytes 172040 | tf_op jit(solution)/shard_map/ppermute | solution.py:277
  11.9 0.2 collective-permute-done
  12.1 2.5 %collective-permute-done.1 = f32[56,256]{1,0:T(8,128)S(1)} collective-permute-done((f32[56,256]{1,0:T(8,128)S(1)}, f32[56,256]{1,0:T(8,128)S(1)}, u32[]{:S(2)}, u32[]{:S(2)}) %collective-permute-start.1) | collective-permute-done | bytes 57376 | tf_op jit(solution)/shard_map/ppermute | solution.py:277
  14.6 0.3 collective-permute-done.2
  14.9 1.1 %collective-permute-start.3 = (f32[4,56,256]{2,1,0:T(8,128)S(1)}, f32[4,56,256]{2,1,0:T(8,128)S(1)}, u32[]{:S(2)}, u32[]{:S(2)}) collective-permute-start(f32[4,56,256]{2,1,0:T(8,128)S(1)} %pad_maximum_fusion), channel_id=1, source_target_pairs={{0,2},{2,0},{1,3},{3,1},{4,6},{6,4},{5,7},{7,5},{8,10},{10,8},{9,1... | collective-permute-start | bytes 688136 | tf_op jit(solution)/shard_map/ppermute | solution.py:284
  16.0 4.5 %collective-permute-done.3 = f32[4,56,256]{2,1,0:T(8,128)S(1)} collective-permute-done((f32[4,56,256]{2,1,0:T(8,128)S(1)}, f32[4,56,256]{2,1,0:T(8,128)S(1)}, u32[]{:S(2)}, u32[]{:S(2)}) %collective-permute-start.3) | collective-permute-done | bytes 229408 | tf_op jit(solution)/shard_map/ppermute | solution.py:284
  20.5 2.5 %collective-permute-start.4 = (f32[8,56,256]{2,1,0:T(8,128)S(1)}, f32[8,56,256]{2,1,0:T(8,128)S(1)}, u32[]{:S(2)}, u32[]{:S(2)}) collective-permute-start(f32[8,56,256]{2,1,0:T(8,128)S(1)} %get-tuple-element.2), channel_id=1, source_target_pairs={{0,1},{1,0},{2,3},{3,2},{4,5},{5,4},{6,7},{7,6},{8,9},{9,8},{10,11... | collective-permute-start | bytes 1376264 | tf_op jit(solution)/shard_map/ppermute | solution.py:284
  23.1 0.1 pad_add_fusion.place_ref
  23.1 1.4 %collective-permute-done.4 = f32[8,56,256]{2,1,0:T(8,128)S(1)} collective-permute-done((f32[8,56,256]{2,1,0:T(8,128)S(1)}, f32[8,56,256]{2,1,0:T(8,128)S(1)}, u32[]{:S(2)}, u32[]{:S(2)}) %collective-permute-start.4) | collective-permute-done | bytes 458784 | tf_op jit(solution)/shard_map/ppermute | solution.py:284
  24.5 0.0 copy-start.5
  24.6 0.6 %copy-done.5 = f32[4,4]{1,0:T(4,128)S(1)} copy-done((f32[4,4]{1,0:T(4,128)S(1)}, f32[4,4]{1,0:T(4,128)}, u32[]{:S(2)}) %copy-start.5) | copy-done | bytes 88
  25.2 20.2 %grid_fields.1 = (f32[4,2,64,128]{3,2,1,0:T(8,128)}, f32[3,4,2,64,128]{4,3,2,1,0:T(8,128)}) custom-call(f32[4,4]{1,0:T(4,128)S(1)} %copy-done.5, s32[2]{0:T(128)S(1)} %pad_add_fusion.place_ref, f32[16,56,256]{2,1,0:T(8,128)S(1)} %constant_dynamic-update-slice_fusion.5.lists_ref), custom_call_target="tpu_custom_call" | custom-call | tf_op jit(solution)/shard_map/grid_fields/pallas_call | solution.py:318
  (7 shorter events, 0.1 us)
Async XLA Ops:
  0.6 0.7 %copy-start = (s32[4096,1]{0,1:T(1,128)S(1)}, s32[4096,1]{0,1:T(1,128)}, u32[]{:S(2)}) copy-start(s32[4096,1]{0,1:T(1,128)} %param.6) | copy-start | bytes 49156
  1.3 0.7 %copy-start.1 = (s32[4096]{0:T(1024)S(1)}, s32[4096]{0:T(1024)}, u32[]{:S(2)}) copy-start(s32[4096]{0:T(1024)} %param.7) | copy-start | bytes 49156
  2.1 0.7 %copy-start.2 = (s32[4096]{0:T(1024)S(1)}, s32[4096]{0:T(1024)}, u32[]{:S(2)}) copy-start(s32[4096]{0:T(1024)} %param.8) | copy-start | bytes 49156
  2.8 0.7 %copy-start.3 = (f32[4096]{0:T(1024)S(1)}, f32[4096]{0:T(1024)}, u32[]{:S(2)}) copy-start(f32[4096]{0:T(1024)} %param.9) | copy-start | bytes 49156
  3.5 0.7 %copy-start.4 = (f32[4096]{0:T(1024)S(1)}, f32[4096]{0:T(1024)}, u32[]{:S(2)}) copy-start(f32[4096]{0:T(1024)} %param.10) | copy-start | bytes 49156
  6.3 5.8 %collective-permute-start = (f32[56,256]{1,0:T(8,128)S(1)}, f32[56,256]{1,0:T(8,128)S(1)}, u32[]{:S(2)}, u32[]{:S(2)}) collective-permute-start(f32[56,256]{1,0:T(8,128)S(1)} %sort_beads.1), channel_id=1, source_target_pairs={{0,4},{4,8},{8,12},{12,0},{1,5},{5,9},{9,13},{13,1},{2,6},{6,10},{... | collective-permute-start | bytes 172040 | tf_op jit(solution)/shard_map/ppermute | solution.py:277
  8.5 6.1 %collective-permute-start.1 = (f32[56,256]{1,0:T(8,128)S(1)}, f32[56,256]{1,0:T(8,128)S(1)}, u32[]{:S(2)}, u32[]{:S(2)}) collective-permute-start(f32[56,256]{1,0:T(8,128)S(1)} %sort_beads.1), channel_id=1, source_target_pairs={{0,8},{4,12},{8,0},{12,4},{1,9},{5,13},{9,1},{13,5},{2,10},{6,14},... | collective-permute-start | bytes 172040 | tf_op jit(solution)/shard_map/ppermute | solution.py:277
  10.8 4.1 %collective-permute-start.2 = (f32[56,256]{1,0:T(8,128)S(1)}, f32[56,256]{1,0:T(8,128)S(1)}, u32[]{:S(2)}, u32[]{:S(2)}) collective-permute-start(f32[56,256]{1,0:T(8,128)S(1)} %sort_beads.1), channel_id=1, source_target_pairs={{0,12},{4,0},{8,4},{12,8},{1,13},{5,1},{9,5},{13,9},{2,14},{6,2},{... | collective-permute-start | bytes 172040 | tf_op jit(solution)/shard_map/ppermute | solution.py:277
  14.9 5.6 %collective-permute-start.3 = (f32[4,56,256]{2,1,0:T(8,128)S(1)}, f32[4,56,256]{2,1,0:T(8,128)S(1)}, u32[]{:S(2)}, u32[]{:S(2)}) collective-permute-start(f32[4,56,256]{2,1,0:T(8,128)S(1)} %pad_maximum_fusion), channel_id=1, source_target_pairs={{0,2},{2,0},{1,3},{3,1},{4,6},{6,4},{5,7},{7,5},{8,10},{10,8},{9,1... | collective-permute-start | bytes 688136 | tf_op jit(solution)/shard_map/ppermute | solution.py:284
  20.5 4.0 %collective-permute-start.4 = (f32[8,56,256]{2,1,0:T(8,128)S(1)}, f32[8,56,256]{2,1,0:T(8,128)S(1)}, u32[]{:S(2)}, u32[]{:S(2)}) collective-permute-start(f32[8,56,256]{2,1,0:T(8,128)S(1)} %get-tuple-element.2), channel_id=1, source_target_pairs={{0,1},{1,0},{2,3},{3,2},{4,5},{5,4},{6,7},{7,6},{8,9},{9,8},{10,11... | collective-permute-start | bytes 1376264 | tf_op jit(solution)/shard_map/ppermute | solution.py:284
  24.5 0.7 %copy-start.5 = (f32[4,4]{1,0:T(4,128)S(1)}, f32[4,4]{1,0:T(4,128)}, u32[]{:S(2)}) copy-start(f32[4,4]{1,0:T(4,128)} %chi_ref.1) | copy-start | bytes 196

commit v2 on v0

v2 whole, which is shorter than its diff:
```python
import functools

import jax
import jax.numpy as jnp
from jax import lax
from jax.experimental import pallas as pl
from jax.experimental.pallas import tpu as pltpu
from jax.sharding import PartitionSpec as P

S = 4
X = 256
Y = 128
CZ = 2

compress = 0.5

BUCKET = 8
BUCKETS = X // BUCKET
RIM = 4
LINE = 128
WINDOW = 2 * BUCKET
TARGETS = CZ + 2
META = 8
GROUP = 4

NT = (((1,), (1,)), ((), ()))


def pieces_of(values):
    parts = []
    for _ in range(2):
        part = values.astype(jnp.bfloat16)
        parts.append(part)
        values = values - part.astype(jnp.float32)
    parts.append(values.astype(jnp.bfloat16))
    return parts


def sort_kernel(key_ref, lower_ref, upper_ref, out_ref, left_ref, right_ref):
    lines = key_ref.shape[0]
    places = lines * LINE
    halves = lines // 2
    key = key_ref[...]
    row = (key // Y) & (X - 1)
    bucket = ((row + RIM) & (X - 1)) // BUCKET
    member_iota = lax.broadcasted_iota(jnp.int32, (BUCKETS, LINE), 0)
    members = [
        jnp.where(bucket[i : i + 1, :] == member_iota, 1.0, 0.0) for i in range(lines)
    ]
    stacked = jnp.concatenate([m.astype(jnp.bfloat16) for m in members], 0)
    source = lax.broadcasted_iota(jnp.int32, (LINE, 2 * LINE), 0)
    target = lax.broadcasted_iota(jnp.int32, (LINE, 2 * LINE), 1)
    before = jnp.where(source < target, 1.0, 0.0).astype(jnp.bfloat16)
    counted = jnp.dot(stacked, before, preferred_element_type=jnp.float32)
    total = jnp.zeros((BUCKETS, LINE), jnp.float32)
    ranks = []
    for i in range(lines):
        ranks.append(counted[i * BUCKETS : (i + 1) * BUCKETS, :LINE] + total)
        total = total + counted[i * BUCKETS : (i + 1) * BUCKETS, LINE:]
    start = total
    shift = 1
    while shift < BUCKETS:
        start = start + jnp.where(member_iota >= shift, pltpu.roll(start, shift, 0), 0.0)
        shift *= 2
    start = start - total
    lane = lax.broadcasted_iota(jnp.int32, (BUCKETS, LINE), 1)
    starts = jnp.sum(jnp.where(member_iota == lane, start, 0.0), 0, keepdims=True)
    starts = jnp.where(lane[:1] < BUCKETS, starts, float(places))
    lower, upper = lower_ref[...], upper_ref[...]
    parts = [part.astype(jnp.float32) for part in (key // 65536, (key // 256) & 255, key & 255)]
    parts += [part.astype(jnp.float32) for part in pieces_of(lower) + pieces_of(upper)]
    half_iota = lax.broadcasted_iota(jnp.int32, (halves, LINE), 0)
    slot_iota = lax.broadcasted_iota(jnp.int32, (2 * LINE, LINE), 0)
    for i in range(lines):
        place = jnp.sum(members[i] * (ranks[i] + start), 0, keepdims=True).astype(jnp.int32)
        hit = half_iota == place // (2 * LINE)
        for n, part in enumerate(parts):
            left_ref[n * halves : (n + 1) * halves, i * LINE : (i + 1) * LINE] = jnp.where(
                hit, part[i : i + 1, :], 0.0
            ).astype(jnp.bfloat16)
        right_ref[:, i * LINE : (i + 1) * LINE] = jnp.where(
            slot_iota == (place & (2 * LINE - 1)), 1.0, 0.0
        ).astype(jnp.bfloat16)
    placed = lax.dot_general(
        left_ref[...], right_ref[...], NT, preferred_element_type=jnp.float32
    )

    def part_of(n):
        return placed[n * halves : (n + 1) * halves]

    sorted_values = (
        part_of(0) * 65536.0 + part_of(1) * 256.0 + part_of(2),
        part_of(3) + part_of(4) + part_of(5),
        part_of(6) + part_of(7) + part_of(8),
    )
    for n, value in enumerate(sorted_values):
        out_ref[n * lines : n * lines + halves] = value[:, :LINE]
        out_ref[n * lines + halves : (n + 1) * lines] = value[:, LINE:]
    out_ref[3 * lines : 3 * lines + META] = jnp.broadcast_to(starts, (META, LINE))


def shares_of(lower, upper, height, first, heights):
    shares = (
        0.0625 * lower,
        0.25 * lower + 0.0625 * upper,
        0.375 * lower + 0.25 * upper,
        0.25 * lower + 0.375 * upper,
        0.0625 * lower + 0.25 * upper,
        0.0625 * upper,
    )
    none = jnp.zeros_like(lower)
    if heights == 8:
        turn = (first + 2 + heights - height) & 7
        kept = list(shares) + [none, none]
        for bit, length in ((4, 7), (2, 5), (1, 4)):
            chosen = (turn & bit) != 0
            kept = [
                jnp.where(chosen, kept[(i + bit) % 8], kept[i]) for i in range(length)
            ]
        return kept
    amounts = []
    for n in range(TARGETS):
        above = (first + n + 2 + heights - height) % heights
        amount = none
        for d, share in enumerate(shares):
            amount = jnp.where(above == d, share, amount)
        amounts.append(amount)
    return amounts


def spare_lines(lists):
    return max(2, lists // 4)


def deposit(heights, own_rows, slab, group, lists_ref, first_list, lists, grid_ref, scratch):
    near_ref, column_ref, amount_ref, starts_ref, starts_smem, sem = scratch
    lines = (lists_ref.shape[1] - META) // 3
    places = lines * LINE
    halves = lines // 2
    buckets = own_rows // BUCKET + 1
    windows = -(-buckets // 2)

    starts_ref[0:lists] = lists_ref[first_list : first_list + lists, 3 * lines, :].astype(jnp.int32)
    copy = pltpu.make_async_copy(starts_ref, starts_smem, sem)
    copy.start()
    first_row = group * own_rows - RIM

    def spread(i, carry):
        key = lists_ref[first_list + i, 0:lines, :].astype(jnp.int32)
        lower = lists_ref[first_list + i, lines : 2 * lines, :]
        upper = lists_ref[first_list + i, 2 * lines : 3 * lines, :]
        spot = pl.ds(pl.multiple_of(i * lines, lines), lines)
        plane = key // (X * Y)
        species = plane // heights
        height = plane - species * heights
        row = (key // Y) & (X - 1)
        near_ref[spot, :] = ((row - first_row) & (X - 1)) + (species // 2) * 1024
        column_ref[spot, :] = ((key & (Y - 1)) + (species & 1) * Y).astype(jnp.float32)
        for n, amount in enumerate(shares_of(lower, upper, height, slab * CZ - 1, heights)):
            high = amount.astype(jnp.bfloat16).astype(jnp.float32)
            amount_ref[2 * n, spot, :] = high
            amount_ref[2 * n + 1, spot, :] = amount - high
        return carry

    lax.fori_loop(0, lists, spread, 0, unroll=2)
    copy.wait()

    near_iota = lax.broadcasted_iota(jnp.int32, (2 * WINDOW, LINE), 0)
    near_iota = jnp.where(near_iota >= WINDOW, near_iota + (1024 - WINDOW), near_iota)
    column_iota = lax.broadcasted_iota(jnp.int32, (2 * Y, LINE), 0).astype(jnp.float32).astype(jnp.bfloat16)
    one, zero = jnp.bfloat16(1), jnp.bfloat16(0)

    def operands_of(i, line, base):
        at = pl.ds(i * lines + (line & 1) * halves + ((line & (lines - 1)) >> 1), 1)
        hit = jnp.where(near_ref[at, :] - base == near_iota, 1.0, 0.0).astype(jnp.bfloat16)
        left = [
            hit * jnp.broadcast_to(amount_ref[n, at, :], hit.shape).astype(jnp.bfloat16)
            for n in range(2 * TARGETS)
        ]
        column = jnp.broadcast_to(column_ref[at, :], (2 * Y, LINE)).astype(jnp.bfloat16)
        return jnp.concatenate(left, 0), jnp.where(column == column_iota, one, zero)

    def add_product(window, entries):
        got = 0.0
        for g in range(0, len(entries), GROUP):
            pairs = [operands_of(*entry) for entry in entries[g : g + GROUP]]
            got = got + lax.dot_general(
                jnp.concatenate([pair[0] for pair in pairs], 1),
                jnp.concatenate([pair[1] for pair in pairs], 1),
                NT,
                preferred_element_type=jnp.float32,
            )
        for n in range(TARGETS):
            for half in range(2):
                high = (2 * n * 2 + half) * WINDOW
                low = ((2 * n + 1) * 2 + half) * WINDOW
                rows = slice(window * WINDOW, (window + 1) * WINDOW)
                grid_ref[n, half, rows, :] += got[high : high + WINDOW] + got[low : low + WINDOW]

    never = 8192
    spare = spare_lines(lists)

    def range_of(window):
        usual = min(2, buckets - 2 * window) + 1
        low = group * (own_rows // BUCKET) + 2 * window
        high = low + usual - 1
        wrapped = jnp.where(high > BUCKETS, BUCKETS, 0)
        lead = jnp.where(high > BUCKETS, places, 0)

        def span_of(i):
            begin = starts_smem[i, low]
            end = starts_smem[i, high - wrapped] + lead
            first = begin // LINE
            count = jnp.where(end > begin, (end + (LINE - 1)) // LINE - first, 0)
            return first, jnp.minimum(count, lines)

        return usual, span_of

    flags = []
    for window in range(windows):
        usual, span_of = range_of(window)
        base = window * WINDOW
        spare_list = [jnp.int32(0)] * spare
        spare_line = [jnp.int32(0)] * spare
        spare_base = [jnp.int32(never)] * spare
        used = jnp.int32(0)
        most = jnp.int32(0)
        entries = []
        for i in range(lists):
            first, count = span_of(i)
            for t in range(usual):
                entries.append((i, first + t, jnp.where(t < count, base, never)))
            over = count > usual
            for k in range(spare):
                mine = over & (used == k)
                spare_list[k] = jnp.where(mine, i, spare_list[k])
                spare_line[k] = jnp.where(mine, first + usual, spare_line[k])
                spare_base[k] = jnp.where(mine, base, spare_base[k])
            used = used + jnp.where(over, 1, 0)
            most = jnp.maximum(most, count)
        for k in range(spare):
            entries.append((spare_list[k], spare_line[k], spare_base[k]))
        add_product(window, entries)
        flags.append((used > spare) | (most > usual + 1))

    def rest_of_window(window):
        usual, span_of = range_of(window)
        base = window * WINDOW

        def rest_of(i, before):
            first, count = span_of(i)
            over = count > usual
            done = usual + jnp.where(over & (before < spare), 1, 0)

            def four_lines(turn, carry):
                ahead = [done + turn * 4 + k for k in range(4)]
                add_product(window, [(i, first + t, jnp.where(t < count, base, never)) for t in ahead])
                return carry

            lax.fori_loop(0, (count - done + 3) // 4, four_lines, 0)
            return before + jnp.where(over, 1, 0)

        lax.fori_loop(0, lists, rest_of, jnp.int32(0))

    @pl.when(functools.reduce(jnp.logical_or, flags))
    def _():
        for window in range(windows):
            pl.when(flags[window])(functools.partial(rest_of_window, window))


def fields(own_rows, chi_ref, grid_ref, potential_ref, force_ref):
    rows = own_rows + 2

    def smooth_of(n, b):
        lanes = slice((b % 2) * Y, (b % 2 + 1) * Y)

        def shifted(k):
            return grid_ref[n, b // 2, RIM - 3 + k : RIM - 3 + k + rows, lanes]

        value = (
            0.375 * shifted(2) + 0.25 * (shifted(1) + shifted(3)) + 0.0625 * (shifted(0) + shifted(4))
        )
        close = pltpu.roll(value, 1, 1) + pltpu.roll(value, Y - 1, 1)
        far = pltpu.roll(value, 2, 1) + pltpu.roll(value, Y - 2, 1)
        return 0.375 * value + 0.25 * close + 0.0625 * far

    layers = []
    for n in range(TARGETS):
        smooth = [smooth_of(n, b) for b in range(S)]
        layer = []
        for a in range(S):
            value = -1.0 / compress
            for b in range(S):
                factor = 0.5 * (chi_ref[a, b] + chi_ref[b, a]) + 1.0 / compress
                value = value + factor * smooth[b]
            layer.append(value)
        layers.append(layer)
    for a in range(S):
        for z in range(CZ):
            value = layers[z + 1][a]
            own = value[1:-1]
            potential_ref[a, z] = own
            force_ref[0, a, z] = (layers[z][a][1:-1] - layers[z + 2][a][1:-1]) * 0.5
            force_ref[1, a, z] = (value[:-2] - value[2:]) * 0.5
            force_ref[2, a, z] = (pltpu.roll(own, 1, 1) - pltpu.roll(own, Y - 1, 1)) * 0.5


def grid_kernel(heights, own_rows, lists, chi_ref, place_ref, lists_ref, potential_ref, force_ref, grid_ref, *scratch):
    step = pl.program_id(0)

    @pl.when(step == 0)
    def _():
        grid_ref[...] = jnp.zeros_like(grid_ref)

    deposit(heights, own_rows, place_ref[0], place_ref[1], lists_ref, 0, lists, grid_ref, scratch)

    @pl.when(step == pl.num_programs(0) - 1)
    def _():
        fields(own_rows, chi_ref, grid_ref, potential_ref, force_ref)


def deposit_scratch(lists, lines):
    return [
        pltpu.VMEM((lists * lines, LINE), jnp.int32),
        pltpu.VMEM((lists * lines, LINE), jnp.float32),
        pltpu.VMEM((2 * TARGETS, lists * lines, LINE), jnp.float32),
        pltpu.VMEM((max(lists, 8), LINE), jnp.int32),
        pltpu.SMEM((max(lists, 8), LINE), jnp.int32),
        pltpu.SemaphoreType.DMA,
    ]


def gathered(block):
    slab_count = lax.axis_size("slab")
    if slab_count > 8:
        block = lax.all_gather(block, "slab")
    else:
        turned = [
            lax.ppermute(block, "slab", [(i, (i + k) % slab_count) for i in range(slab_count)])
            for k in range(1, slab_count)
        ]
        block = jnp.stack([block] + turned)
    for axis in ("beads", "sub"):
        count = lax.axis_size(axis)
        turned = [
            lax.ppermute(block, axis, [(i, (i + k) % count) for i in range(count)])
            for k in range(1, count)
        ]
        block = jnp.concatenate([block] + turned)
    return block


def on_device(dest_slab, local_cell, species, bead_mass, rise_fraction, chi_matrix):
    bead_count = local_cell.shape[0]
    slab_count = lax.axis_size("slab")
    group_count = lax.axis_size(("beads", "sub"))
    heights = slab_count * CZ
    own_rows = X // group_count
    scale = CZ * X * Y / (bead_count * group_count)
    lines = bead_count // LINE
    list_lines = 3 * lines + META
    dest, cell, kind, mass, rise = (
        x.reshape(lines, LINE) for x in (dest_slab, local_cell, species, bead_mass, rise_fraction)
    )
    height = dest * CZ + cell // (X * Y)
    key = (kind * heights + height) * (X * Y) + (cell & (X * Y - 1))
    lower = mass * scale * (1.0 - rise)
    upper = mass * scale * rise
    vmem = pl.BlockSpec(memory_space=pltpu.VMEM)
    smem = pl.BlockSpec(memory_space=pltpu.SMEM)
    block = pl.pallas_call(
        sort_kernel,
        out_shape=jax.ShapeDtypeStruct((list_lines, LINE), jnp.float32),
        in_specs=[vmem] * 3,
        out_specs=vmem,
        scratch_shapes=[
            pltpu.VMEM((9 * lines // 2, bead_count), jnp.bfloat16),
            pltpu.VMEM((2 * LINE, bead_count), jnp.bfloat16),
        ],
        compiler_params=pltpu.CompilerParams(vmem_limit_bytes=32 << 20),
        name="sort_beads",
    )(key, lower, upper)
    lists = gathered(block)
    place = jnp.stack([lax.axis_index("slab"), lax.axis_index(("beads", "sub"))]).astype(jnp.int32)
    together = 16
    windows = -(-(own_rows // BUCKET + 1) // 2)
    potential, force = pl.pallas_call(
        functools.partial(grid_kernel, heights, own_rows, together),
        grid=(lists.shape[0] // together,),
        out_shape=(
            jax.ShapeDtypeStruct((S, CZ, own_rows, Y), jnp.float32),
            jax.ShapeDtypeStruct((3, S, CZ, own_rows, Y), jnp.float32),
        ),
        in_specs=[
            smem,
            smem,
            pl.BlockSpec((together, list_lines, LINE), lambda i: (i, 0, 0)),
        ],
        out_specs=(
            pl.BlockSpec((S, CZ, own_rows, Y), lambda i: (0, 0, 0, 0)),
            pl.BlockSpec((3, S, CZ, own_rows, Y), lambda i: (0, 0, 0, 0, 0)),
        ),
        scratch_shapes=[
            pltpu.VMEM((TARGETS, 2, windows * WINDOW, 2 * Y), jnp.float32),
        ]
        + deposit_scratch(together, lines),
        compiler_params=pltpu.CompilerParams(vmem_limit_bytes=48 << 20),
        name="grid_fields",
    )(chi_matrix, place, lists)
    return (potential, force)


def solution(mesh):
    placed = (
        P(("runs", "slab", "beads", "sub"), None),
        P(("runs", "slab", "beads", "sub")),
        P(("runs", "slab", "beads", "sub")),
        P(("runs", "slab", "beads", "sub")),
        P(("runs", "slab", "beads", "sub")),
        P(),
    )
    return jax.shard_map(
        on_device,
        mesh=mesh,
        in_specs=placed,
        out_specs=(
            P("runs", "slab", ("beads", "sub"), None),
            P(None, "runs", "slab", ("beads", "sub"), None),
        ),
        check_vma=False,
    )
```

time: 314 us -> 31.7 us (0.10)
  other arithmetic: 99 us -> 0.86 us
  local copies, waits for them, and re-layouts: 99.6 us -> 1.46 us
  waiting for transfers between devices: 79 us -> 9.07 us
  between operations: 14.3 us -> 0.74 us
  starting transfers between devices: 21.2 us -> 8.76 us
  Pallas kernels: 0 us -> 10.3 us
    scatter-add x3 -> x0, other arithmetic: 89.7 us -> none  [the longest x1 45 us: on_device(): partial_value.at[flat_index + plane_cells].add(got_amounts[1].reshape(-1))]
    reduce_scatter x1 -> x0, waiting for transfers between devices: 48.6 us -> none  [on_device(): lax.psum_scatter(partial_value, ('beads', 'sub'), scatter_dimension=2, ti...]
    gather x2 -> x0, local copies, waits for them, and re-layouts: 46.1 us -> none  [the longest x1 23 us: on_device(): sorted_target = target[bead_order]]
    scatter x2 -> x0, local copies, waits for them, and re-layouts: 42.9 us -> none  [the longest x1 26.8 us: on_device(): jnp.zeros((2, slab_count * capacity), jnp.float32).at[:, slot_index]]
    ppermute x9 -> x5, waiting for transfers between devices: 24.7 us -> 9.07 us  [the longest x2 6.16 us: gathered(): lax.ppermute(block, axis, [(i, (i + k) % count) for i in range(count)])]
    all_to_all x2 -> x0, starting transfers between devices: 11.4 us -> none  [the longest x1 6.32 us: on_device(): lax.all_to_all(send_index, 'slab', split_axis=1, concat_axis=1, tiled=True)]
    pallas_call x0 -> x2, Pallas kernels: none -> 10.3 us  [the longest x1 8.21 us: on_device(): pl.pallas_call(functools.partial(grid_kernel, heights, own_rows, together...]
    sort x1 -> x0, other arithmetic: 6.55 us -> none  [on_device(): bead_order = jnp.argsort(target, stable=True)]
  transfers between devices with their start and end apart: 12 -> 5, of which waited for: 10 -> 5; matrix products, arithmetic and copies ran while one was open for 11% -> 0% of each run, Pallas kernels for 0% -> 0%
where the time goes in v2:
time: 31.7 us; the launch traced here: 31.2 us
  Pallas kernels  10.3 us (32%)
  waiting for transfers between devices  9.07 us (29%)
  starting transfers between devices  8.76 us (28%)
  local copies, waits for them, and re-layouts  1.46 us (5%)
  other arithmetic  0.86 us (3%)
  between operations  0.74 us (2%)
    pallas_call x1, Pallas kernels, on_device(): pl.pallas_call(functools.partial(grid_kernel, heights, own_rows, together...  8.21 us
    ppermute x3, starting transfers between devices, gathered(): lax.ppermute(block, 'slab', [(i, (i + k) % slab_count) for i in range(sla...  7 us
    ppermute x2, waiting for transfers between devices, gathered(): lax.ppermute(block, axis, [(i, (i + k) % count) for i in range(count)])  6.16 us
    ppermute x3, waiting for transfers between devices, gathered(): lax.ppermute(block, 'slab', [(i, (i + k) % slab_count) for i in range(sla...  2.91 us
    pallas_call x1, Pallas kernels, on_device(): pl.pallas_call(sort_kernel, out_shape=jax.ShapeDtypeStruct((list_lines, L...  2.05 us
    ppermute x2, starting transfers between devices, gathered(): lax.ppermute(block, axis, [(i, (i + k) % count) for i in range(count)])  1.76 us
    unnamed x14, local copies, waits for them, and re-layouts  1.4 us
    mul x1, other arithmetic, on_device(): height = dest * CZ + cell // (X * Y)  0.74 us
  transfers between devices with their start and end apart: 5, of which 5 were waited for; matrix products, arithmetic and copies ran while one was open for 0% of the time, Pallas kernels for 0%

profile of v2, /device:TPU:0, one launch (start us, length us, event | category | flops | bytes accessed | tf_op | source)
XLA Modules:
  0.0 31.2 jit_solution(6015307468354733823)
XLA Ops:
  0.6 0.0 copy-start.1
  0.6 0.0 copy-start.2
  0.6 0.7 %broadcast_multiply_fusion = s32[4096,1]{0,1:T(1,128)S(1)} fusion(s32[4096,1]{0,1:T(1,128)} %param.6), kind=kLoop, calls=%fused_computation.29 | loop fusion | flops 4096 | bytes 32768 | tf_op jit(solution)/shard_map/mul | solution.py:365
  1.4 0.0 copy-done.1
  1.4 0.0 copy-done.2
  1.4 0.0 copy-start.3
  1.4 0.0 copy-start.4
  1.5 0.7 %copy-done.3 = s32[4096]{0:T(1024)S(1)} copy-done((s32[4096]{0:T(1024)S(1)}, s32[4096]{0:T(1024)}, u32[]{:S(2)}) %copy-start.3) | copy-done | bytes 16408
  2.1 0.0 copy-done.4
  2.2 2.1 %sort_beads.1 = f32[104,128]{1,0:T(8,128)S(1)} custom-call(s32[32,128]{1,0:T(8,128)S(1)} %fusion.4.key_ref, f32[32,128]{1,0:T(8,128)S(1)} %get-tuple-element.13.lower_ref, f32[32,128]{1,0:T(8,128)S(1)} %get-tuple-element.12.upper_ref), custom_call_target="tpu_custom_call" | custom-call | tf_op jit(solution)/shard_map/sort_beads/pallas_call | solution.py:371
  4.2 3.1 %collective-permute-start = (f32[104,128]{1,0:T(8,128)S(1)}, f32[104,128]{1,0:T(8,128)S(1)}, u32[]{:S(2)}, u32[]{:S(2)}) collective-permute-start(f32[104,128]{1,0:T(8,128)S(1)} %sort_beads.1), channel_id=1, source_target_pairs={{0,4},{4,8},{8,12},{12,0},{1,5},{5,9},{9,13},{13,1},{2,6},{6,10},{... | collective-permute-start | bytes 159752 | tf_op jit(solution)/shard_map/ppermute | solution.py:339
  7.3 2.6 %collective-permute-start.1 = (f32[104,128]{1,0:T(8,128)S(1)}, f32[104,128]{1,0:T(8,128)S(1)}, u32[]{:S(2)}, u32[]{:S(2)}) collective-permute-start(f32[104,128]{1,0:T(8,128)S(1)} %sort_beads.1), channel_id=1, source_target_pairs={{0,8},{4,12},{8,0},{12,4},{1,9},{5,13},{9,1},{13,5},{2,10},{6,14},... | collective-permute-start | bytes 159752 | tf_op jit(solution)/shard_map/ppermute | solution.py:339
  9.9 1.3 %collective-permute-start.2 = (f32[104,128]{1,0:T(8,128)S(1)}, f32[104,128]{1,0:T(8,128)S(1)}, u32[]{:S(2)}, u32[]{:S(2)}) collective-permute-start(f32[104,128]{1,0:T(8,128)S(1)} %sort_beads.1), channel_id=1, source_target_pairs={{0,12},{4,0},{8,4},{12,8},{1,13},{5,1},{9,5},{13,9},{2,14},{6,2},{... | collective-permute-start | bytes 159752 | tf_op jit(solution)/shard_map/ppermute | solution.py:339
  11.2 0.3 %collective-permute-done = f32[104,128]{1,0:T(8,128)S(1)} collective-permute-done((f32[104,128]{1,0:T(8,128)S(1)}, f32[104,128]{1,0:T(8,128)S(1)}, u32[]{:S(2)}, u32[]{:S(2)}) %collective-permute-start) | collective-permute-done | bytes 53280 | tf_op jit(solution)/shard_map/ppermute | solution.py:339
  11.6 2.1 %collective-permute-done.1 = f32[104,128]{1,0:T(8,128)S(1)} collective-permute-done((f32[104,128]{1,0:T(8,128)S(1)}, f32[104,128]{1,0:T(8,128)S(1)}, u32[]{:S(2)}, u32[]{:S(2)}) %collective-permute-start.1) | collective-permute-done | bytes 53280 | tf_op jit(solution)/shard_map/ppermute | solution.py:339
  13.7 0.4 %collective-permute-done.2 = f32[104,128]{1,0:T(8,128)S(1)} collective-permute-done((f32[104,128]{1,0:T(8,128)S(1)}, f32[104,128]{1,0:T(8,128)S(1)}, u32[]{:S(2)}, u32[]{:S(2)}) %collective-permute-start.2) | collective-permute-done | bytes 53280 | tf_op jit(solution)/shard_map/ppermute | solution.py:339
  14.2 1.7 %collective-permute-start.3 = (f32[4,104,128]{2,1,0:T(8,128)S(1)}, f32[4,104,128]{2,1,0:T(8,128)S(1)}, u32[]{:S(2)}, u32[]{:S(2)}) collective-permute-start(f32[4,104,128]{2,1,0:T(8,128)S(1)} %pad_maximum_fusion), channel_id=1, source_target_pairs={{0,2},{2,0},{1,3},{3,1},{4,6},{6,4},{5,7},{7,5},{8,10},{10,8},{9,1... | collective-permute-start | bytes 638984 | tf_op jit(solution)/shard_map/ppermute | solution.py:346
  15.9 4.5 %collective-permute-done.3 = f32[4,104,128]{2,1,0:T(8,128)S(1)} collective-permute-done((f32[4,104,128]{2,1,0:T(8,128)S(1)}, f32[4,104,128]{2,1,0:T(8,128)S(1)}, u32[]{:S(2)}, u32[]{:S(2)}) %collective-permute-start.3) | collective-permute-done | bytes 213024 | tf_op jit(solution)/shard_map/ppermute | solution.py:346
  20.4 0.1 collective-permute-start.4
  20.5 0.1 pad_add_fusion.place_ref
  20.6 1.7 %collective-permute-done.4 = f32[8,104,128]{2,1,0:T(8,128)S(1)} collective-permute-done((f32[8,104,128]{2,1,0:T(8,128)S(1)}, f32[8,104,128]{2,1,0:T(8,128)S(1)}, u32[]{:S(2)}, u32[]{:S(2)}) %collective-permute-start.4) | collective-permute-done | bytes 426016 | tf_op jit(solution)/shard_map/ppermute | solution.py:346
  22.3 0.0 copy-start
  22.3 0.6 %copy-done = f32[4,4]{1,0:T(4,128)S(1)} copy-done((f32[4,4]{1,0:T(4,128)S(1)}, f32[4,4]{1,0:T(4,128)}, u32[]{:S(2)}) %copy-start) | copy-done | bytes 88
  22.9 8.2 %grid_fields.1 = (f32[4,2,64,128]{3,2,1,0:T(8,128)}, f32[3,4,2,64,128]{4,3,2,1,0:T(8,128)}) custom-call(f32[4,4]{1,0:T(4,128)S(1)} %copy-done, s32[2]{0:T(128)S(1)} %pad_add_fusion.place_ref, f32[16,104,128]{2,1,0:T(8,128)S(1)} %constant_dynamic-update-slice_fusion.5.lists_ref), custom_call_target="tpu_custom_call" | custom-call | tf_op jit(solution)/shard_map/grid_fields/pallas_call | solution.py:387
  (9 shorter events, 0.1 us)
Async XLA Ops:
  0.6 0.8 %copy-start.1 = (f32[4096]{0:T(1024)S(1)}, f32[4096]{0:T(1024)}, u32[]{:S(2)}) copy-start(f32[4096]{0:T(1024)} %param.10) | copy-start | bytes 49156
  0.6 0.8 %copy-start.2 = (f32[4096]{0:T(1024)S(1)}, f32[4096]{0:T(1024)}, u32[]{:S(2)}) copy-start(f32[4096]{0:T(1024)} %param.9) | copy-start | bytes 49156
  1.4 0.7 %copy-start.3 = (s32[4096]{0:T(1024)S(1)}, s32[4096]{0:T(1024)}, u32[]{:S(2)}) copy-start(s32[4096]{0:T(1024)} %param.7) | copy-start | bytes 49156
  1.4 0.7 %copy-start.4 = (s32[4096]{0:T(1024)S(1)}, s32[4096]{0:T(1024)}, u32[]{:S(2)}) copy-start(s32[4096]{0:T(1024)} %param.8) | copy-start | bytes 49156
  4.2 7.3 %collective-permute-start = (f32[104,128]{1,0:T(8,128)S(1)}, f32[104,128]{1,0:T(8,128)S(1)}, u32[]{:S(2)}, u32[]{:S(2)}) collective-permute-start(f32[104,128]{1,0:T(8,128)S(1)} %sort_beads.1), channel_id=1, source_target_pairs={{0,4},{4,8},{8,12},{12,0},{1,5},{5,9},{9,13},{13,1},{2,6},{6,10},{... | collective-permute-start | bytes 159752 | tf_op jit(solution)/shard_map/ppermute | solution.py:339
  7.3 6.4 %collective-permute-start.1 = (f32[104,128]{1,0:T(8,128)S(1)}, f32[104,128]{1,0:T(8,128)S(1)}, u32[]{:S(2)}, u32[]{:S(2)}) collective-permute-start(f32[104,128]{1,0:T(8,128)S(1)} %sort_beads.1), channel_id=1, source_target_pairs={{0,8},{4,12},{8,0},{12,4},{1,9},{5,13},{9,1},{13,5},{2,10},{6,14},... | collective-permute-start | bytes 159752 | tf_op jit(solution)/shard_map/ppermute | solution.py:339
  9.9 4.3 %collective-permute-start.2 = (f32[104,128]{1,0:T(8,128)S(1)}, f32[104,128]{1,0:T(8,128)S(1)}, u32[]{:S(2)}, u32[]{:S(2)}) collective-permute-start(f32[104,128]{1,0:T(8,128)S(1)} %sort_beads.1), channel_id=1, source_target_pairs={{0,12},{4,0},{8,4},{12,8},{1,13},{5,1},{9,5},{13,9},{2,14},{6,2},{... | collective-permute-start | bytes 159752 | tf_op jit(solution)/shard_map/ppermute | solution.py:339
  14.2 6.2 %collective-permute-start.3 = (f32[4,104,128]{2,1,0:T(8,128)S(1)}, f32[4,104,128]{2,1,0:T(8,128)S(1)}, u32[]{:S(2)}, u32[]{:S(2)}) collective-permute-start(f32[4,104,128]{2,1,0:T(8,128)S(1)} %pad_maximum_fusion), channel_id=1, source_target_pairs={{0,2},{2,0},{1,3},{3,1},{4,6},{6,4},{5,7},{7,5},{8,10},{10,8},{9,1... | collective-permute-start | bytes 638984 | tf_op jit(solution)/shard_map/ppermute | solution.py:346
  20.4 1.8 %collective-permute-start.4 = (f32[8,104,128]{2,1,0:T(8,128)S(1)}, f32[8,104,128]{2,1,0:T(8,128)S(1)}, u32[]{:S(2)}, u32[]{:S(2)}) collective-permute-start(f32[8,104,128]{2,1,0:T(8,128)S(1)} %get-tuple-element.2), channel_id=1, source_target_pairs={{0,1},{1,0},{2,3},{3,2},{4,5},{5,4},{6,7},{7,6},{8,9},{9,8},{10,11... | collective-permute-start | bytes 1277960 | tf_op jit(solution)/shard_map/ppermute | solution.py:346
  22.3 0.7 %copy-start = (f32[4,4]{1,0:T(4,128)S(1)}, f32[4,4]{1,0:T(4,128)}, u32[]{:S(2)}) copy-start(f32[4,4]{1,0:T(4,128)} %chi_ref.1) | copy-start | bytes 196

commit v3 on v2

--- a/solution.py
+++ b/solution.py
@@ -22,6 +22,7 @@
 TARGETS = CZ + 2
 META = 8
 GROUP = 4
+SORT_GROUP = 2
 
 NT = (((1,), (1,)), ((), ()))
 
@@ -36,12 +37,21 @@
     return parts
 
 
-def sort_kernel(key_ref, lower_ref, upper_ref, out_ref, left_ref, right_ref):
-    lines = key_ref.shape[0]
+def sort_kernel(heights, scale, *refs):
+    sources, out_ref, targets, sems = refs[:5], refs[5], refs[6:11], refs[11]
+    copies = [
+        pltpu.make_async_copy(source, target, sems.at[i])
+        for i, (source, target) in enumerate(zip(sources, targets))
+    ]
+    for copy in copies:
+        copy.start()
+    dest_ref, cell_ref, species_ref, mass_ref, rise_ref = targets
+    lines = cell_ref.shape[0]
     places = lines * LINE
     halves = lines // 2
-    key = key_ref[...]
-    row = (key // Y) & (X - 1)
+    copies[1].wait()
+    cell = cell_ref[...]
+    row = (cell // Y) & (X - 1)
     bucket = ((row + RIM) & (X - 1)) // BUCKET
     member_iota = lax.broadcasted_iota(jnp.int32, (BUCKETS, LINE), 0)
     members = [
@@ -66,24 +76,33 @@
     lane = lax.broadcasted_iota(jnp.int32, (BUCKETS, LINE), 1)
     starts = jnp.sum(jnp.where(member_iota == lane, start, 0.0), 0, keepdims=True)
     starts = jnp.where(lane[:1] < BUCKETS, starts, float(places))
-    lower, upper = lower_ref[...], upper_ref[...]
+    for i in (0, 2, 3, 4):
+        copies[i].wait()
+    height = dest_ref[...] * CZ + cell // (X * Y)
+    key = (species_ref[...] * heights + height) * (X * Y) + (cell & (X * Y - 1))
+    mass = mass_ref[...] * scale
+    lower = mass * (1.0 - rise_ref[...])
+    upper = mass * rise_ref[...]
     parts = [part.astype(jnp.float32) for part in (key // 65536, (key // 256) & 255, key & 255)]
     parts += [part.astype(jnp.float32) for part in pieces_of(lower) + pieces_of(upper)]
     half_iota = lax.broadcasted_iota(jnp.int32, (halves, LINE), 0)
     slot_iota = lax.broadcasted_iota(jnp.int32, (2 * LINE, LINE), 0)
-    for i in range(lines):
-        place = jnp.sum(members[i] * (ranks[i] + start), 0, keepdims=True).astype(jnp.int32)
-        hit = half_iota == place // (2 * LINE)
-        for n, part in enumerate(parts):
-            left_ref[n * halves : (n + 1) * halves, i * LINE : (i + 1) * LINE] = jnp.where(
-                hit, part[i : i + 1, :], 0.0
-            ).astype(jnp.bfloat16)
-        right_ref[:, i * LINE : (i + 1) * LINE] = jnp.where(
-            slot_iota == (place & (2 * LINE - 1)), 1.0, 0.0
-        ).astype(jnp.bfloat16)
-    placed = lax.dot_general(
-        left_ref[...], right_ref[...], NT, preferred_element_type=jnp.float32
-    )
+    placed = 0.0
+    for first in range(0, lines, SORT_GROUP):
+        lefts, rights = [], []
+        for i in range(first, first + SORT_GROUP):
+            place = jnp.sum(members[i] * (ranks[i] + start), 0, keepdims=True).astype(jnp.int32)
+            hit = half_iota == place // (2 * LINE)
+            lefts.append(
+                jnp.concatenate([jnp.where(hit, part[i : i + 1, :], 0.0) for part in parts], 0)
+            )
+            rights.append(jnp.where(slot_iota == (place & (2 * LINE - 1)), 1.0, 0.0))
+        placed = placed + lax.dot_general(
+            jnp.concatenate(lefts, 1).astype(jnp.bfloat16),
+            jnp.concatenate(rights, 1).astype(jnp.bfloat16),
+            NT,
+            preferred_element_type=jnp.float32,
+        )
 
     def part_of(n):
         return placed[n * halves : (n + 1) * halves]
@@ -132,23 +151,24 @@
     return max(2, lists // 4)
 
 
-def deposit(heights, own_rows, slab, group, lists_ref, first_list, lists, grid_ref, scratch):
+def deposit(heights, own_rows, slab, group, lists_ref, before_ref, grid_ref, scratch):
     near_ref, column_ref, amount_ref, starts_ref, starts_smem, sem = scratch
+    lists = lists_ref.shape[0]
     lines = (lists_ref.shape[1] - META) // 3
     places = lines * LINE
     halves = lines // 2
     buckets = own_rows // BUCKET + 1
     windows = -(-buckets // 2)
 
-    starts_ref[0:lists] = lists_ref[first_list : first_list + lists, 3 * lines, :].astype(jnp.int32)
+    starts_ref[0:lists] = lists_ref[:, 3 * lines, :].astype(jnp.int32)
     copy = pltpu.make_async_copy(starts_ref, starts_smem, sem)
     copy.start()
     first_row = group * own_rows - RIM
 
     def spread(i, carry):
-        key = lists_ref[first_list + i, 0:lines, :].astype(jnp.int32)
-        lower = lists_ref[first_list + i, lines : 2 * lines, :]
-        upper = lists_ref[first_list + i, 2 * lines : 3 * lines, :]
+        key = lists_ref[i, 0:lines, :].astype(jnp.int32)
+        lower = lists_ref[i, lines : 2 * lines, :]
+        upper = lists_ref[i, 2 * lines : 3 * lines, :]
         spot = pl.ds(pl.multiple_of(i * lines, lines), lines)
         plane = key // (X * Y)
         species = plane // heights
@@ -180,7 +200,7 @@
         column = jnp.broadcast_to(column_ref[at, :], (2 * Y, LINE)).astype(jnp.bfloat16)
         return jnp.concatenate(left, 0), jnp.where(column == column_iota, one, zero)
 
-    def add_product(window, entries):
+    def add_product(window, entries, base_ref):
         got = 0.0
         for g in range(0, len(entries), GROUP):
             pairs = [operands_of(*entry) for entry in entries[g : g + GROUP]]
@@ -195,7 +215,10 @@
                 high = (2 * n * 2 + half) * WINDOW
                 low = ((2 * n + 1) * 2 + half) * WINDOW
                 rows = slice(window * WINDOW, (window + 1) * WINDOW)
-                grid_ref[n, half, rows, :] += got[high : high + WINDOW] + got[low : low + WINDOW]
+                value = got[high : high + WINDOW] + got[low : low + WINDOW]
+                if base_ref is not None:
+                    value = value + base_ref[n, half, rows, :]
+                grid_ref[n, half, rows, :] = value
 
     never = 8192
     spare = spare_lines(lists)
@@ -240,7 +263,7 @@
             most = jnp.maximum(most, count)
         for k in range(spare):
             entries.append((spare_list[k], spare_line[k], spare_base[k]))
-        add_product(window, entries)
+        add_product(window, entries, before_ref)
         flags.append((used > spare) | (most > usual + 1))
 
     def rest_of_window(window):
@@ -254,7 +277,8 @@
 
             def four_lines(turn, carry):
                 ahead = [done + turn * 4 + k for k in range(4)]
-                add_product(window, [(i, first + t, jnp.where(t < count, base, never)) for t in ahead])
+                entries = [(i, first + t, jnp.where(t < count, base, never)) for t in ahead]
+                add_product(window, entries, grid_ref)
                 return carry
 
             lax.fori_loop(0, (count - done + 3) // 4, four_lines, 0)
@@ -268,7 +292,9 @@
             pl.when(flags[window])(functools.partial(rest_of_window, window))
 
 
-def fields(own_rows, chi_ref, grid_ref, potential_ref, force_ref):
+def fields(
+    own_rows, chi_ref, grid_ref, potential_ref, force_ref, potential_hbm, force_hbm, sems
+):
     rows = own_rows + 2
 
     def smooth_of(n, b):
@@ -284,39 +310,121 @@
         far = pltpu.roll(value, 2, 1) + pltpu.roll(value, Y - 2, 1)
         return 0.375 * value + 0.25 * close + 0.0625 * far
 
-    layers = []
-    for n in range(TARGETS):
-        smooth = [smooth_of(n, b) for b in range(S)]
-        layer = []
-        for a in range(S):
+    factors = [
+        [0.5 * (chi_ref[a, b] + chi_ref[b, a]) + 1.0 / compress for b in range(S)] for a in range(S)
+    ]
+    smooth = [[smooth_of(n, b) for b in range(S)] for n in range(TARGETS)]
+    copies = []
+    for a in range(S):
+        layers = []
+        for n in range(TARGETS):
             value = -1.0 / compress
             for b in range(S):
-                factor = 0.5 * (chi_ref[a, b] + chi_ref[b, a]) + 1.0 / compress
-                value = value + factor * smooth[b]
-            layer.append(value)
-        layers.append(layer)
-    for a in range(S):
+                value = value + factors[a][b] * smooth[n][b]
+            layers.append(value)
         for z in range(CZ):
-            value = layers[z + 1][a]
+            value = layers[z + 1]
             own = value[1:-1]
             potential_ref[a, z] = own
-            force_ref[0, a, z] = (layers[z][a][1:-1] - layers[z + 2][a][1:-1]) * 0.5
+            force_ref[0, a, z] = (layers[z][1:-1] - layers[z + 2][1:-1]) * 0.5
             force_ref[1, a, z] = (value[:-2] - value[2:]) * 0.5
             force_ref[2, a, z] = (pltpu.roll(own, 1, 1) - pltpu.roll(own, Y - 1, 1)) * 0.5
-
-
-def grid_kernel(heights, own_rows, lists, chi_ref, place_ref, lists_ref, potential_ref, force_ref, grid_ref, *scratch):
-    step = pl.program_id(0)
-
-    @pl.when(step == 0)
-    def _():
-        grid_ref[...] = jnp.zeros_like(grid_ref)
-
-    deposit(heights, own_rows, place_ref[0], place_ref[1], lists_ref, 0, lists, grid_ref, scratch)
-
-    @pl.when(step == pl.num_programs(0) - 1)
-    def _():
-        fields(own_rows, chi_ref, grid_ref, potential_ref, force_ref)
+            at = 1 + 2 * (a * CZ + z)
+            copies += [
+                pltpu.make_async_copy(potential_ref.at[a, z], potential_hbm.at[a, z], sems.at[at]),
+                pltpu.make_async_copy(force_ref.at[:, a, z], force_hbm.at[:, a, z], sems.at[at + 1]),
+            ]
+            copies[-2].start()
+            copies[-1].start()
+    for copy in copies:
+        copy.wait()
+
+
+def part_kernel(heights, own_rows, role, *refs):
+    step = pl.program_id(0) if role.steps > 1 else 0
+    refs = list(refs)
+    chi_hbm = refs.pop(0) if role.last else None
+    lists_ref = refs.pop(0)
+    before_ref = None if role.first else refs.pop(0)
+    if role.last:
+        potential_ref, force_ref = refs.pop(0), refs.pop(0)
+    grid_ref = refs.pop(0)
+    if role.last:
+        chi_ref, potential_vmem, force_vmem, sems = refs[:4]
+        del refs[:4]
+        chi_copy = pltpu.make_async_copy(chi_hbm, chi_ref, sems.at[0])
+        pl.when(step == 0)(chi_copy.start)
+
+    if role.steps > 1:
+
+        @pl.when(step == 0)
+        def _():
+            grid_ref[...] = jnp.zeros_like(grid_ref) if role.first else before_ref[...]
+
+        before_ref = grid_ref
+
+    deposit(heights, own_rows, lax.axis_index("slab"), lax.axis_index(("beads", "sub")), lists_ref, before_ref, grid_ref, refs)
+
+    if role.last:
+
+        @pl.when(step == role.steps - 1)
+        def _():
+            chi_copy.wait()
+            fields(
+                own_rows, chi_ref, grid_ref, potential_vmem, force_vmem, potential_ref, force_ref, sems
+            )
+
+
+class Role:
+    def __init__(self, first, last, steps):
+        self.first, self.last, self.steps = first, last, steps
+
+
+def deposit_call(heights, own_rows, lists, before, chi):
+    total, list_lines, _ = lists.shape
+    lines = (list_lines - META) // 3
+    together = min(8, total)
+    role = Role(before is None, chi is not None, total // together)
+    whole = pl.BlockSpec(memory_space=pltpu.VMEM)
+    hbm = pl.BlockSpec(memory_space=pl.ANY)
+    windows = -(-(own_rows // BUCKET + 1) // 2)
+    grid_shape = (TARGETS, 2, windows * WINDOW, 2 * Y)
+    operands, specs = [], []
+    if role.last:
+        operands.append(pltpu.with_memory_space_constraint(chi, pltpu.MemorySpace.HBM))
+        specs.append(hbm)
+    operands.append(lists)
+    specs.append(
+        whole if role.steps == 1 else pl.BlockSpec((together, list_lines, LINE), lambda i: (i, 0, 0))
+    )
+    if not role.first:
+        operands.append(before)
+        specs.append(whole)
+    scratch = deposit_scratch(together, lines)
+    if role.last:
+        shapes = ((S, CZ, own_rows, Y), (3, S, CZ, own_rows, Y))
+        out_shape = tuple(jax.ShapeDtypeStruct(shape, jnp.float32) for shape in shapes)
+        out_specs = (hbm, hbm)
+        scratch = [
+            pltpu.VMEM(grid_shape, jnp.float32),
+            pltpu.SMEM((S, S), jnp.float32),
+            pltpu.VMEM(shapes[0], jnp.float32),
+            pltpu.VMEM(shapes[1], jnp.float32),
+            pltpu.SemaphoreType.DMA((1 + 2 * S * CZ,)),
+        ] + scratch
+    else:
+        out_shape = jax.ShapeDtypeStruct(grid_shape, jnp.float32)
+        out_specs = whole
+    return pl.pallas_call(
+        functools.partial(part_kernel, heights, own_rows, role),
+        grid=(role.steps,),
+        out_shape=out_shape,
+        in_specs=specs,
+        out_specs=out_specs,
+        scratch_shapes=scratch,
+        compiler_params=pltpu.CompilerParams(vmem_limit_bytes=40 << 20),
+        name="grid_fields" if role.last else "deposit_first" if role.first else "deposit_more",
+    )(*operands)
 
 
 def deposit_scratch(lists, lines):
@@ -330,24 +438,9 @@
     ]
 
 
-def gathered(block):
-    slab_count = lax.axis_size("slab")
-    if slab_count > 8:
-        block = lax.all_gather(block, "slab")
-    else:
-        turned = [
-            lax.ppermute(block, "slab", [(i, (i + k) % slab_count) for i in range(slab_count)])
-            for k in range(1, slab_count)
-        ]
-        block = jnp.stack([block] + turned)
-    for axis in ("beads", "sub"):
-        count = lax.axis_size(axis)
-        turned = [
-            lax.ppermute(block, axis, [(i, (i + k) % count) for i in range(count)])
-            for k in range(1, count)
-        ]
-        block = jnp.concatenate([block] + turned)
-    return block
+def turned(block, axis, by):
+    count = lax.axis_size(axis)
+    return lax.ppermute(block, axis, [(i, (i + by) % count) for i in range(count)])
 
 
 def on_device(dest_slab, local_cell, species, bead_mass, rise_fraction, chi_matrix):
@@ -359,55 +452,35 @@
     scale = CZ * X * Y / (bead_count * group_count)
     lines = bead_count // LINE
     list_lines = 3 * lines + META
-    dest, cell, kind, mass, rise = (
-        x.reshape(lines, LINE) for x in (dest_slab, local_cell, species, bead_mass, rise_fraction)
-    )
-    height = dest * CZ + cell // (X * Y)
-    key = (kind * heights + height) * (X * Y) + (cell & (X * Y - 1))
-    lower = mass * scale * (1.0 - rise)
-    upper = mass * scale * rise
     vmem = pl.BlockSpec(memory_space=pltpu.VMEM)
-    smem = pl.BlockSpec(memory_space=pltpu.SMEM)
+    beads = [
+        pltpu.with_memory_space_constraint(x.reshape(lines, LINE), pltpu.MemorySpace.HBM)
+        for x in (dest_slab, local_cell, species, bead_mass, rise_fraction)
+    ]
     block = pl.pallas_call(
-        sort_kernel,
+        functools.partial(sort_kernel, heights, scale),
         out_shape=jax.ShapeDtypeStruct((list_lines, LINE), jnp.float32),
-        in_specs=[vmem] * 3,
+        in_specs=[pl.BlockSpec(memory_space=pl.ANY)] * 5,
         out_specs=vmem,
-        scratch_shapes=[
-            pltpu.VMEM((9 * lines // 2, bead_count), jnp.bfloat16),
-            pltpu.VMEM((2 * LINE, bead_count), jnp.bfloat16),
-        ],
+        scratch_shapes=[pltpu.VMEM((lines, LINE), x.dtype) for x in beads]
+        + [pltpu.SemaphoreType.DMA((5,))],
         compiler_params=pltpu.CompilerParams(vmem_limit_bytes=32 << 20),
         name="sort_beads",
-    )(key, lower, upper)
-    lists = gathered(block)
-    place = jnp.stack([lax.axis_index("slab"), lax.axis_index(("beads", "sub"))]).astype(jnp.int32)
-    together = 16
-    windows = -(-(own_rows // BUCKET + 1) // 2)
-    potential, force = pl.pallas_call(
-        functools.partial(grid_kernel, heights, own_rows, together),
-        grid=(lists.shape[0] // together,),
-        out_shape=(
-            jax.ShapeDtypeStruct((S, CZ, own_rows, Y), jnp.float32),
-            jax.ShapeDtypeStruct((3, S, CZ, own_rows, Y), jnp.float32),
-        ),
-        in_specs=[
-            smem,
-            smem,
-            pl.BlockSpec((together, list_lines, LINE), lambda i: (i, 0, 0)),
-        ],
-        out_specs=(
-            pl.BlockSpec((S, CZ, own_rows, Y), lambda i: (0, 0, 0, 0)),
-            pl.BlockSpec((3, S, CZ, own_rows, Y), lambda i: (0, 0, 0, 0, 0)),
-        ),
-        scratch_shapes=[
-            pltpu.VMEM((TARGETS, 2, windows * WINDOW, 2 * Y), jnp.float32),
-        ]
-        + deposit_scratch(together, lines),
-        compiler_params=pltpu.CompilerParams(vmem_limit_bytes=48 << 20),
-        name="grid_fields",
-    )(chi_matrix, place, lists)
-    return (potential, force)
+    )(*beads)
+    if slab_count > 8:
+        column = [lax.all_gather(block, "slab")]
+    else:
+        steps = sorted(range(1, slab_count), key=lambda k: min(k, slab_count - k))
+        column = [x[None] for x in [block] + [turned(block, "slab", k) for k in steps]]
+    others = [turned(x, "beads", k) for k in range(1, lax.axis_size("beads")) for x in column]
+    column = jnp.concatenate(column)
+    others = jnp.concatenate(others)
+    grid = deposit_call(heights, own_rows, column, None, None)
+    half = jnp.concatenate([column, others])
+    half, grid = lax.optimization_barrier((half, grid))
+    far = jnp.concatenate([turned(half, "sub", k) for k in range(1, lax.axis_size("sub"))])
+    grid = deposit_call(heights, own_rows, others, grid, None)
+    return deposit_call(heights, own_rows, far, grid, chi_matrix)
 
 
 def solution(mesh):

time: 31.7 us -> 25.8 us (0.81); the launches traced: 31.2 us -> 25.9 us
  waiting for transfers between devices: 9.07 us -> 2.25 us
  starting transfers between devices: 8.76 us -> 11.3 us
  local copies, waits for them, and re-layouts: 1.46 us -> 0.04 us
  Pallas kernels: 10.3 us -> 11.6 us
  other arithmetic: 0.86 us -> 0.04 us
    ppermute x5 -> x8, waiting for transfers between devices: 9.07 us -> 2.25 us  [turned(): lax.ppermute(block, axis, [(i, (i + by) % count) for i in range(count)])]
    ppermute x5 -> x8, starting transfers between devices: 8.76 us -> 11.3 us  [turned(): lax.ppermute(block, axis, [(i, (i + by) % count) for i in range(count)])]
    unnamed x14 -> x7, local copies, waits for them, and re-layouts: 1.4 us -> 0.04 us
    pallas_call x2 -> x4, Pallas kernels: 10.3 us -> 11.6 us  [the longest x3 9.4 us: deposit_call(): pl.pallas_call(functools.partial(part_kernel, heights, own_rows, role), g...]
    mul x2 -> x0, other arithmetic: 0.75 us -> none  [the longest x1 0.74 us: on_device(): height = dest * CZ + cell // (X * Y)]
  transfers between devices with their start and end apart: 5 -> 8, of which waited for: 5 -> 2; matrix products, arithmetic and copies ran while one was open for 0% -> 0% of each run, Pallas kernels for 0% -> 15%
where the time goes in v3:
time: 25.8 us; the launch traced here: 25.9 us
  Pallas kernels  11.6 us (45%)
  starting transfers between devices  11.3 us (44%)
  waiting for transfers between devices  2.25 us (9%)
  between operations  0.74 us (3%)
    ppermute x8, starting transfers between devices, turned(): lax.ppermute(block, axis, [(i, (i + by) % count) for i in range(count)])  11.3 us
    pallas_call x3, Pallas kernels, deposit_call(): pl.pallas_call(functools.partial(part_kernel, heights, own_rows, role), g...  9.4 us
    ppermute x8, waiting for transfers between devices, turned(): lax.ppermute(block, axis, [(i, (i + by) % count) for i in range(count)])  2.25 us
    pallas_call x1, Pallas kernels, on_device(): pl.pallas_call(functools.partial(sort_kernel, heights, scale), out_shape=...  2.2 us
  transfers between devices with their start and end apart: 8, of which 2 were waited for; matrix products, arithmetic and copies ran while one was open for 0% of the time, Pallas kernels for 15%

profile of v3, /device:TPU:0, one launch (start us, length us, event | category | flops | bytes accessed | tf_op | source)
XLA Modules:
  0.0 25.9 jit_solution(9505909077631819030)
XLA Ops:
  0.6 2.2 %sort_beads.1 = f32[104,128]{1,0:T(8,128)S(1)} custom-call(s32[32,128]{1,0:T(8,128)} %bitcast.21, s32[32,128]{1,0:T(8,128)} %bitcast.22, s32[32,128]{1,0:T(8,128)} %bitcast.23, f32[32,128]{1,0:T(8,128)} %bitcast.24, f32[32,128]{1,0:T(8,128)} %bitcast.25), custom_call_target="tpu_custom_call" | custom-call | tf_op jit(solution)/shard_map/sort_beads/pallas_call | solution.py:460
  2.8 4.1 %collective-permute-start.2 = (f32[104,128]{1,0:T(8,128)S(1)}, f32[104,128]{1,0:T(8,128)S(1)}, u32[]{:S(2)}, u32[]{:S(2)}) collective-permute-start(f32[104,128]{1,0:T(8,128)S(1)} %sort_beads.1), channel_id=1, source_target_pairs={{0,8},{4,12},{8,0},{12,4},{1,9},{5,13},{9,1},{13,5},{2,10},{6,14},... | collective-permute-start | bytes 159752 | tf_op jit(solution)/shard_map/ppermute | solution.py:443
  6.9 1.4 %collective-permute-start.1 = (f32[104,128]{1,0:T(8,128)S(1)}, f32[104,128]{1,0:T(8,128)S(1)}, u32[]{:S(2)}, u32[]{:S(2)}) collective-permute-start(f32[104,128]{1,0:T(8,128)S(1)} %sort_beads.1), channel_id=1, source_target_pairs={{0,12},{4,0},{8,4},{12,8},{1,13},{5,1},{9,5},{13,9},{2,14},{6,2},{... | collective-permute-start | bytes 159752 | tf_op jit(solution)/shard_map/ppermute | solution.py:443
  8.3 0.7 %collective-permute-start = (f32[104,128]{1,0:T(8,128)S(1)}, f32[104,128]{1,0:T(8,128)S(1)}, u32[]{:S(2)}, u32[]{:S(2)}) collective-permute-start(f32[104,128]{1,0:T(8,128)S(1)} %sort_beads.1), channel_id=1, source_target_pairs={{0,4},{4,8},{8,12},{12,0},{1,5},{5,9},{9,13},{13,1},{2,6},{6,10},{... | collective-permute-start | bytes 159752 | tf_op jit(solution)/shard_map/ppermute | solution.py:443
  9.0 1.5 %collective-permute-start.3 = (f32[1,104,128]{2,1,0:T(8,128)S(1)}, f32[1,104,128]{2,1,0:T(8,128)S(1)}, u32[]{:S(2)}, u32[]{:S(2)}) collective-permute-start(f32[1,104,128]{2,1,0:T(8,128)S(1)} %bitcast.13), channel_id=1, source_target_pairs={{0,2},{2,0},{1,3},{3,1},{4,6},{6,4},{5,7},{7,5},{8,10},{10,8},{9,1... | collective-permute-start | bytes 159752 | tf_op jit(solution)/shard_map/ppermute | solution.py:443
  10.5 0.0 collective-permute-done.2
  10.5 1.0 %collective-permute-start.6 = (f32[1,104,128]{2,1,0:T(8,128)S(1)}, f32[1,104,128]{2,1,0:T(8,128)S(1)}, u32[]{:S(2)}, u32[]{:S(2)}) collective-permute-start(f32[1,104,128]{2,1,0:T(8,128)S(1)} %bitcast.15), channel_id=1, source_target_pairs={{0,2},{2,0},{1,3},{3,1},{4,6},{6,4},{5,7},{7,5},{8,10},{10,8},{9,1... | collective-permute-start | bytes 159752 | tf_op jit(solution)/shard_map/ppermute | solution.py:443
  11.4 0.0 collective-permute-done.1
  11.4 1.1 %collective-permute-start.5 = (f32[1,104,128]{2,1,0:T(8,128)S(1)}, f32[1,104,128]{2,1,0:T(8,128)S(1)}, u32[]{:S(2)}, u32[]{:S(2)}) collective-permute-start(f32[1,104,128]{2,1,0:T(8,128)S(1)} %bitcast.17), channel_id=1, source_target_pairs={{0,2},{2,0},{1,3},{3,1},{4,6},{6,4},{5,7},{7,5},{8,10},{10,8},{9,1... | collective-permute-start | bytes 159752 | tf_op jit(solution)/shard_map/ppermute | solution.py:443
  12.6 1.7 %collective-permute-done = f32[104,128]{1,0:T(8,128)S(1)} collective-permute-done((f32[104,128]{1,0:T(8,128)S(1)}, f32[104,128]{1,0:T(8,128)S(1)}, u32[]{:S(2)}, u32[]{:S(2)}) %collective-permute-start) | collective-permute-done | bytes 53280 | tf_op jit(solution)/shard_map/ppermute | solution.py:443
  14.2 1.5 %collective-permute-start.4 = (f32[1,104,128]{2,1,0:T(8,128)S(1)}, f32[1,104,128]{2,1,0:T(8,128)S(1)}, u32[]{:S(2)}, u32[]{:S(2)}) collective-permute-start(f32[1,104,128]{2,1,0:T(8,128)S(1)} %bitcast.19), channel_id=1, source_target_pairs={{0,2},{2,0},{1,3},{3,1},{4,6},{6,4},{5,7},{7,5},{8,10},{10,8},{9,1... | collective-permute-start | bytes 159752 | tf_op jit(solution)/shard_map/ppermute | solution.py:443
  15.8 0.0 collective-permute-done.3
  15.8 2.0 %deposit_first.1.refs_1_ = f32[4,2,80,256]{3,2,1,0:T(8,128)S(1)} custom-call(f32[4,104,128]{2,1,0:T(8,128)S(1)} %pad_maximum_fusion.refs_0_), custom_call_target="tpu_custom_call" | custom-call | tf_op jit(solution)/shard_map/deposit_first/pallas_call | solution.py:418
  17.8 0.6 %collective-permute-done.4 = f32[1,104,128]{2,1,0:T(8,128)S(1)} collective-permute-done((f32[1,104,128]{2,1,0:T(8,128)S(1)}, f32[1,104,128]{2,1,0:T(8,128)S(1)}, u32[]{:S(2)}, u32[]{:S(2)}) %collective-permute-start.4) | collective-permute-done | bytes 53280 | tf_op jit(solution)/shard_map/ppermute | solution.py:443
  18.4 0.0 collective-permute-done.5
  18.4 0.0 collective-permute-done.6
  18.4 0.1 collective-permute-start.7
  18.5 2.0 %deposit_more.1.refs_2_ = f32[4,2,80,256]{3,2,1,0:T(8,128)S(1)} custom-call(f32[4,104,128]{2,1,0:T(8,128)S(1)} %pad_maximum_fusion.1.refs_0_, f32[4,2,80,256]{3,2,1,0:T(8,128)S(1)} %deposit_first.1.refs_1_), custom_call_target="tpu_custom_call" | custom-call | tf_op jit(solution)/shard_map/deposit_more/pallas_call | solution.py:418
  20.5 0.0 collective-permute-done.7.refs_1_
  20.5 5.4 %grid_fields.1 = (f32[4,2,64,128]{3,2,1,0:T(8,128)}, f32[3,4,2,64,128]{4,3,2,1,0:T(8,128)}) custom-call(f32[4,4]{1,0:T(4,128)} %refs_0_.1, f32[8,104,128]{2,1,0:T(8,128)S(1)} %collective-permute-done.7.refs_1_, f32[4,2,80,256]{3,2,1,0:T(8,128)S(1)} %deposit_more.1.refs_2_), custom_call_target="tpu_custom_call" | custom-call | tf_op jit(solution)/shard_map/grid_fields/pallas_call | solution.py:418
  (10 shorter events, 0.1 us)
Async XLA Ops:
  2.8 7.6 %collective-permute-start.2 = (f32[104,128]{1,0:T(8,128)S(1)}, f32[104,128]{1,0:T(8,128)S(1)}, u32[]{:S(2)}, u32[]{:S(2)}) collective-permute-start(f32[104,128]{1,0:T(8,128)S(1)} %sort_beads.1), channel_id=1, source_target_pairs={{0,8},{4,12},{8,0},{12,4},{1,9},{5,13},{9,1},{13,5},{2,10},{6,14},... | collective-permute-start | bytes 159752 | tf_op jit(solution)/shard_map/ppermute | solution.py:443
  6.9 4.5 %collective-permute-start.1 = (f32[104,128]{1,0:T(8,128)S(1)}, f32[104,128]{1,0:T(8,128)S(1)}, u32[]{:S(2)}, u32[]{:S(2)}) collective-permute-start(f32[104,128]{1,0:T(8,128)S(1)} %sort_beads.1), channel_id=1, source_target_pairs={{0,12},{4,0},{8,4},{12,8},{1,13},{5,1},{9,5},{13,9},{2,14},{6,2},{... | collective-permute-start | bytes 159752 | tf_op jit(solution)/shard_map/ppermute | solution.py:443
  8.3 5.9 %collective-permute-start = (f32[104,128]{1,0:T(8,128)S(1)}, f32[104,128]{1,0:T(8,128)S(1)}, u32[]{:S(2)}, u32[]{:S(2)}) collective-permute-start(f32[104,128]{1,0:T(8,128)S(1)} %sort_beads.1), channel_id=1, source_target_pairs={{0,4},{4,8},{8,12},{12,0},{1,5},{5,9},{9,13},{13,1},{2,6},{6,10},{... | collective-permute-start | bytes 159752 | tf_op jit(solution)/shard_map/ppermute | solution.py:443
  9.0 6.8 %collective-permute-start.3 = (f32[1,104,128]{2,1,0:T(8,128)S(1)}, f32[1,104,128]{2,1,0:T(8,128)S(1)}, u32[]{:S(2)}, u32[]{:S(2)}) collective-permute-start(f32[1,104,128]{2,1,0:T(8,128)S(1)} %bitcast.13), channel_id=1, source_target_pairs={{0,2},{2,0},{1,3},{3,1},{4,6},{6,4},{5,7},{7,5},{8,10},{10,8},{9,1... | collective-permute-start | bytes 159752 | tf_op jit(solution)/shard_map/ppermute | solution.py:443
  10.5 7.9 %collective-permute-start.6 = (f32[1,104,128]{2,1,0:T(8,128)S(1)}, f32[1,104,128]{2,1,0:T(8,128)S(1)}, u32[]{:S(2)}, u32[]{:S(2)}) collective-permute-start(f32[1,104,128]{2,1,0:T(8,128)S(1)} %bitcast.15), channel_id=1, source_target_pairs={{0,2},{2,0},{1,3},{3,1},{4,6},{6,4},{5,7},{7,5},{8,10},{10,8},{9,1... | collective-permute-start | bytes 159752 | tf_op jit(solution)/shard_map/ppermute | solution.py:443
  11.4 6.9 %collective-permute-start.5 = (f32[1,104,128]{2,1,0:T(8,128)S(1)}, f32[1,104,128]{2,1,0:T(8,128)S(1)}, u32[]{:S(2)}, u32[]{:S(2)}) collective-permute-start(f32[1,104,128]{2,1,0:T(8,128)S(1)} %bitcast.17), channel_id=1, source_target_pairs={{0,2},{2,0},{1,3},{3,1},{4,6},{6,4},{5,7},{7,5},{8,10},{10,8},{9,1... | collective-permute-start | bytes 159752 | tf_op jit(solution)/shard_map/ppermute | solution.py:443
  14.2 4.1 %collective-permute-start.4 = (f32[1,104,128]{2,1,0:T(8,128)S(1)}, f32[1,104,128]{2,1,0:T(8,128)S(1)}, u32[]{:S(2)}, u32[]{:S(2)}) collective-permute-start(f32[1,104,128]{2,1,0:T(8,128)S(1)} %bitcast.19), channel_id=1, source_target_pairs={{0,2},{2,0},{1,3},{3,1},{4,6},{6,4},{5,7},{7,5},{8,10},{10,8},{9,1... | collective-permute-start | bytes 159752 | tf_op jit(solution)/shard_map/ppermute | solution.py:443
  18.4 2.1 %collective-permute-start.7 = (f32[8,104,128]{2,1,0:T(8,128)S(1)}, f32[8,104,128]{2,1,0:T(8,128)S(1)}, u32[]{:S(2)}, u32[]{:S(2)}) collective-permute-start(f32[8,104,128]{2,1,0:T(8,128)S(1)} %constant_dynamic-update-slice_fusion), channel_id=1, source_target_pairs={{0,1},{1,0},{2,3},{3,2},{4,5},{5,4},{6,7},{7,6},{8,9},{9,8},{10,11... | collective-permute-start | bytes 1277960 | tf_op jit(solution)/shard_map/ppermute | solution.py:443

commit v4 on v3

--- a/solution.py
+++ b/solution.py
@@ -57,16 +57,19 @@
     members = [
         jnp.where(bucket[i : i + 1, :] == member_iota, 1.0, 0.0) for i in range(lines)
     ]
-    stacked = jnp.concatenate([m.astype(jnp.bfloat16) for m in members], 0)
-    source = lax.broadcasted_iota(jnp.int32, (LINE, 2 * LINE), 0)
-    target = lax.broadcasted_iota(jnp.int32, (LINE, 2 * LINE), 1)
+    pairs = [jnp.concatenate(members[i : i + 2], 1) for i in range(0, lines, 2)]
+    stacked = jnp.concatenate(pairs, 0).astype(jnp.bfloat16)
+    source = lax.broadcasted_iota(jnp.int32, (2 * LINE, 3 * LINE), 0)
+    target = lax.broadcasted_iota(jnp.int32, (2 * LINE, 3 * LINE), 1)
     before = jnp.where(source < target, 1.0, 0.0).astype(jnp.bfloat16)
     counted = jnp.dot(stacked, before, preferred_element_type=jnp.float32)
     total = jnp.zeros((BUCKETS, LINE), jnp.float32)
     ranks = []
-    for i in range(lines):
-        ranks.append(counted[i * BUCKETS : (i + 1) * BUCKETS, :LINE] + total)
-        total = total + counted[i * BUCKETS : (i + 1) * BUCKETS, LINE:]
+    for i in range(lines // 2):
+        rows = slice(i * BUCKETS, (i + 1) * BUCKETS)
+        ranks.append(counted[rows, :LINE] + total)
+        ranks.append(counted[rows, LINE : 2 * LINE] + total)
+        total = total + counted[rows, 2 * LINE :]
     start = total
     shift = 1
     while shift < BUCKETS:
@@ -86,7 +89,8 @@
     parts = [part.astype(jnp.float32) for part in (key // 65536, (key // 256) & 255, key & 255)]
     parts += [part.astype(jnp.float32) for part in pieces_of(lower) + pieces_of(upper)]
     half_iota = lax.broadcasted_iota(jnp.int32, (halves, LINE), 0)
-    slot_iota = lax.broadcasted_iota(jnp.int32, (2 * LINE, LINE), 0)
+    slot_iota = lax.broadcasted_iota(jnp.int32, (2 * LINE, LINE), 0).astype(jnp.float32).astype(jnp.bfloat16)
+    one, zero = jnp.bfloat16(1), jnp.bfloat16(0)
     placed = 0.0
     for first in range(0, lines, SORT_GROUP):
         lefts, rights = [], []
@@ -96,10 +100,11 @@
             lefts.append(
                 jnp.concatenate([jnp.where(hit, part[i : i + 1, :], 0.0) for part in parts], 0)
             )
-            rights.append(jnp.where(slot_iota == (place & (2 * LINE - 1)), 1.0, 0.0))
+            slot = jnp.broadcast_to((place & (2 * LINE - 1)).astype(jnp.float32), (2 * LINE, LINE))
+            rights.append(jnp.where(slot.astype(jnp.bfloat16) == slot_iota, one, zero))
         placed = placed + lax.dot_general(
             jnp.concatenate(lefts, 1).astype(jnp.bfloat16),
-            jnp.concatenate(rights, 1).astype(jnp.bfloat16),
+            jnp.concatenate(rights, 1),
             NT,
             preferred_element_type=jnp.float32,
         )
@@ -148,7 +153,7 @@
 
 
 def spare_lines(lists):
-    return max(2, lists // 4)
+    return max(2, lists // 2)
 
 
 def deposit(heights, own_rows, slab, group, lists_ref, before_ref, grid_ref, scratch):
@@ -293,7 +298,7 @@
 
 
 def fields(
-    own_rows, chi_ref, grid_ref, potential_ref, force_ref, potential_hbm, force_hbm, sems
+    own_rows, chi_ref, grid_ref, layer_ref, potential_ref, force_ref, potential_hbm, force_hbm, sems
 ):
     rows = own_rows + 2
 
@@ -316,26 +321,27 @@
     smooth = [[smooth_of(n, b) for b in range(S)] for n in range(TARGETS)]
     copies = []
     for a in range(S):
-        layers = []
         for n in range(TARGETS):
             value = -1.0 / compress
             for b in range(S):
                 value = value + factors[a][b] * smooth[n][b]
-            layers.append(value)
+            layer_ref[a, n, 0:rows] = value
         for z in range(CZ):
-            value = layers[z + 1]
-            own = value[1:-1]
+            own = layer_ref[a, z + 1, 1 : 1 + own_rows]
             potential_ref[a, z] = own
-            force_ref[0, a, z] = (layers[z][1:-1] - layers[z + 2][1:-1]) * 0.5
-            force_ref[1, a, z] = (value[:-2] - value[2:]) * 0.5
+            force_ref[0, a, z] = (
+                layer_ref[a, z, 1 : 1 + own_rows] - layer_ref[a, z + 2, 1 : 1 + own_rows]
+            ) * 0.5
+            force_ref[1, a, z] = (
+                layer_ref[a, z + 1, 0:own_rows] - layer_ref[a, z + 1, 2 : 2 + own_rows]
+            ) * 0.5
             force_ref[2, a, z] = (pltpu.roll(own, 1, 1) - pltpu.roll(own, Y - 1, 1)) * 0.5
-            at = 1 + 2 * (a * CZ + z)
-            copies += [
-                pltpu.make_async_copy(potential_ref.at[a, z], potential_hbm.at[a, z], sems.at[at]),
-                pltpu.make_async_copy(force_ref.at[:, a, z], force_hbm.at[:, a, z], sems.at[at + 1]),
-            ]
-            copies[-2].start()
-            copies[-1].start()
+        copies += [
+            pltpu.make_async_copy(potential_ref.at[a], potential_hbm.at[a], sems.at[1 + 2 * a]),
+            pltpu.make_async_copy(force_ref.at[:, a], force_hbm.at[:, a], sems.at[2 + 2 * a]),
+        ]
+        copies[-2].start()
+        copies[-1].start()
     for copy in copies:
         copy.wait()
 
@@ -350,8 +356,8 @@
         potential_ref, force_ref = refs.pop(0), refs.pop(0)
     grid_ref = refs.pop(0)
     if role.last:
-        chi_ref, potential_vmem, force_vmem, sems = refs[:4]
-        del refs[:4]
+        chi_ref, layer_ref, potential_vmem, force_vmem, sems = refs[:5]
+        del refs[:5]
         chi_copy = pltpu.make_async_copy(chi_hbm, chi_ref, sems.at[0])
         pl.when(step == 0)(chi_copy.start)
 
@@ -371,7 +377,7 @@
         def _():
             chi_copy.wait()
             fields(
-                own_rows, chi_ref, grid_ref, potential_vmem, force_vmem, potential_ref, force_ref, sems
+                own_rows, chi_ref, grid_ref, layer_ref, potential_vmem, force_vmem, potential_ref, force_ref, sems
             )
 
 
@@ -383,7 +389,7 @@
 def deposit_call(heights, own_rows, lists, before, chi):
     total, list_lines, _ = lists.shape
     lines = (list_lines - META) // 3
-    together = min(8, total)
+    together = max(n for n in range(1, 9) if total % n == 0)
     role = Role(before is None, chi is not None, total // together)
     whole = pl.BlockSpec(memory_space=pltpu.VMEM)
     hbm = pl.BlockSpec(memory_space=pl.ANY)
@@ -408,9 +414,10 @@
         scratch = [
             pltpu.VMEM(grid_shape, jnp.float32),
             pltpu.SMEM((S, S), jnp.float32),
+            pltpu.VMEM((S, TARGETS, own_rows + 8, Y), jnp.float32),
             pltpu.VMEM(shapes[0], jnp.float32),
             pltpu.VMEM(shapes[1], jnp.float32),
-            pltpu.SemaphoreType.DMA((1 + 2 * S * CZ,)),
+            pltpu.SemaphoreType.DMA((1 + 2 * S,)),
         ] + scratch
     else:
         out_shape = jax.ShapeDtypeStruct(grid_shape, jnp.float32)
@@ -470,16 +477,16 @@
     if slab_count > 8:
         column = [lax.all_gather(block, "slab")]
     else:
-        steps = sorted(range(1, slab_count), key=lambda k: min(k, slab_count - k))
+        steps = sorted(range(1, slab_count), key=lambda k: (-min(k, slab_count - k), -k))
         column = [x[None] for x in [block] + [turned(block, "slab", k) for k in steps]]
     others = [turned(x, "beads", k) for k in range(1, lax.axis_size("beads")) for x in column]
-    column = jnp.concatenate(column)
-    others = jnp.concatenate(others)
-    grid = deposit_call(heights, own_rows, column, None, None)
-    half = jnp.concatenate([column, others])
+    early = jnp.concatenate(column + others[:1])
+    late = jnp.concatenate(others[1:])
+    grid = deposit_call(heights, own_rows, early, None, None)
+    half = jnp.concatenate([early, late])
     half, grid = lax.optimization_barrier((half, grid))
     far = jnp.concatenate([turned(half, "sub", k) for k in range(1, lax.axis_size("sub"))])
-    grid = deposit_call(heights, own_rows, others, grid, None)
+    grid = deposit_call(heights, own_rows, late, grid, None)
     return deposit_call(heights, own_rows, far, grid, chi_matrix)
 
 

time: 25.8 us -> 24.7 us (0.957); the launches traced: 25.9 us -> 24.5 us
  waiting for transfers between devices: 2.25 us -> 1.04 us
    ppermute x8, waiting for transfers between devices: 2.25 us -> 1.04 us  [turned(): lax.ppermute(block, axis, [(i, (i + by) % count) for i in range(count)])]
  transfers between devices with their start and end apart: 8 -> 8, of which waited for: 2 -> 2; matrix products, arithmetic and copies ran while one was open for 0% -> 0% of each run, Pallas kernels for 15% -> 17%
where the time goes in v4:
time: 24.7 us; the launch traced here: 24.5 us
  Pallas kernels  11.4 us (46%)
  starting transfers between devices  11.3 us (46%)
  waiting for transfers between devices  1.04 us (4%)
  between operations  0.76 us (3%)
    ppermute x8, starting transfers between devices, turned(): lax.ppermute(block, axis, [(i, (i + by) % count) for i in range(count)])  11.3 us
    pallas_call x3, Pallas kernels, deposit_call(): pl.pallas_call(functools.partial(part_kernel, heights, own_rows, role), g...  9.16 us
    pallas_call x1, Pallas kernels, on_device(): pl.pallas_call(functools.partial(sort_kernel, heights, scale), out_shape=...  2.22 us
    ppermute x8, waiting for transfers between devices, turned(): lax.ppermute(block, axis, [(i, (i + by) % count) for i in range(count)])  1.04 us
  transfers between devices with their start and end apart: 8, of which 2 were waited for; matrix products, arithmetic and copies ran while one was open for 0% of the time, Pallas kernels for 17%

profile of v4, /device:TPU:0, one launch (start us, length us, event | category | flops | bytes accessed | tf_op | source)
XLA Modules:
  0.0 24.5 jit_solution(12161997036405449609)
XLA Ops:
  0.6 2.2 %sort_beads.1 = f32[104,128]{1,0:T(8,128)S(1)} custom-call(s32[32,128]{1,0:T(8,128)} %bitcast.21, s32[32,128]{1,0:T(8,128)} %bitcast.22, s32[32,128]{1,0:T(8,128)} %bitcast.23, f32[32,128]{1,0:T(8,128)} %bitcast.24, f32[32,128]{1,0:T(8,128)} %bitcast.25), custom_call_target="tpu_custom_call" | custom-call | tf_op jit(solution)/shard_map/sort_beads/pallas_call | solution.py:467
  2.9 3.1 %collective-permute-start.2 = (f32[104,128]{1,0:T(8,128)S(1)}, f32[104,128]{1,0:T(8,128)S(1)}, u32[]{:S(2)}, u32[]{:S(2)}) collective-permute-start(f32[104,128]{1,0:T(8,128)S(1)} %sort_beads.1), channel_id=1, source_target_pairs={{0,4},{4,8},{8,12},{12,0},{1,5},{5,9},{9,13},{13,1},{2,6},{6,10},{... | collective-permute-start | bytes 159752 | tf_op jit(solution)/shard_map/ppermute | solution.py:450
  5.9 2.1 %collective-permute-start.1 = (f32[104,128]{1,0:T(8,128)S(1)}, f32[104,128]{1,0:T(8,128)S(1)}, u32[]{:S(2)}, u32[]{:S(2)}) collective-permute-start(f32[104,128]{1,0:T(8,128)S(1)} %sort_beads.1), channel_id=1, source_target_pairs={{0,12},{4,0},{8,4},{12,8},{1,13},{5,1},{9,5},{13,9},{2,14},{6,2},{... | collective-permute-start | bytes 159752 | tf_op jit(solution)/shard_map/ppermute | solution.py:450
  8.0 0.9 %collective-permute-start = (f32[104,128]{1,0:T(8,128)S(1)}, f32[104,128]{1,0:T(8,128)S(1)}, u32[]{:S(2)}, u32[]{:S(2)}) collective-permute-start(f32[104,128]{1,0:T(8,128)S(1)} %sort_beads.1), channel_id=1, source_target_pairs={{0,8},{4,12},{8,0},{12,4},{1,9},{5,13},{9,1},{13,5},{2,10},{6,14},... | collective-permute-start | bytes 159752 | tf_op jit(solution)/shard_map/ppermute | solution.py:450
  9.0 1.5 %collective-permute-start.3 = (f32[1,104,128]{2,1,0:T(8,128)S(1)}, f32[1,104,128]{2,1,0:T(8,128)S(1)}, u32[]{:S(2)}, u32[]{:S(2)}) collective-permute-start(f32[1,104,128]{2,1,0:T(8,128)S(1)} %bitcast.17), channel_id=1, source_target_pairs={{0,2},{2,0},{1,3},{3,1},{4,6},{6,4},{5,7},{7,5},{8,10},{10,8},{9,1... | collective-permute-start | bytes 159752 | tf_op jit(solution)/shard_map/ppermute | solution.py:450
  10.5 0.0 collective-permute-done.2
  10.5 1.6 %collective-permute-start.6 = (f32[1,104,128]{2,1,0:T(8,128)S(1)}, f32[1,104,128]{2,1,0:T(8,128)S(1)}, u32[]{:S(2)}, u32[]{:S(2)}) collective-permute-start(f32[1,104,128]{2,1,0:T(8,128)S(1)} %bitcast.18), channel_id=1, source_target_pairs={{0,2},{2,0},{1,3},{3,1},{4,6},{6,4},{5,7},{7,5},{8,10},{10,8},{9,1... | collective-permute-start | bytes 159752 | tf_op jit(solution)/shard_map/ppermute | solution.py:450
  12.0 0.0 collective-permute-done.1
  12.1 0.5 %collective-permute-start.5 = (f32[1,104,128]{2,1,0:T(8,128)S(1)}, f32[1,104,128]{2,1,0:T(8,128)S(1)}, u32[]{:S(2)}, u32[]{:S(2)}) collective-permute-start(f32[1,104,128]{2,1,0:T(8,128)S(1)} %bitcast.19), channel_id=1, source_target_pairs={{0,2},{2,0},{1,3},{3,1},{4,6},{6,4},{5,7},{7,5},{8,10},{10,8},{9,1... | collective-permute-start | bytes 159752 | tf_op jit(solution)/shard_map/ppermute | solution.py:450
  12.6 0.8 %collective-permute-done = f32[104,128]{1,0:T(8,128)S(1)} collective-permute-done((f32[104,128]{1,0:T(8,128)S(1)}, f32[104,128]{1,0:T(8,128)S(1)}, u32[]{:S(2)}, u32[]{:S(2)}) %collective-permute-start) | collective-permute-done | bytes 53280 | tf_op jit(solution)/shard_map/ppermute | solution.py:450
  13.4 1.5 %collective-permute-start.4 = (f32[1,104,128]{2,1,0:T(8,128)S(1)}, f32[1,104,128]{2,1,0:T(8,128)S(1)}, u32[]{:S(2)}, u32[]{:S(2)}) collective-permute-start(f32[1,104,128]{2,1,0:T(8,128)S(1)} %bitcast.20), channel_id=1, source_target_pairs={{0,2},{2,0},{1,3},{3,1},{4,6},{6,4},{5,7},{7,5},{8,10},{10,8},{9,1... | collective-permute-start | bytes 159752 | tf_op jit(solution)/shard_map/ppermute | solution.py:450
  14.9 0.0 collective-permute-done.3
  15.0 2.3 %deposit_first.1.refs_1_ = f32[4,2,80,256]{3,2,1,0:T(8,128)S(1)} custom-call(f32[5,104,128]{2,1,0:T(8,128)S(1)} %get-tuple-element.6.refs_0_), custom_call_target="tpu_custom_call" | custom-call | tf_op jit(solution)/shard_map/deposit_first/pallas_call | solution.py:425
  17.3 0.2 collective-permute-done.4
  17.5 0.0 collective-permute-done.5
  17.5 0.0 collective-permute-done.6
  17.6 0.1 collective-permute-start.7
  17.7 1.8 %deposit_more.1.refs_2_ = f32[4,2,80,256]{3,2,1,0:T(8,128)S(1)} custom-call(f32[3,104,128]{2,1,0:T(8,128)S(1)} %pad_maximum_fusion.refs_0_, f32[4,2,80,256]{3,2,1,0:T(8,128)S(1)} %deposit_first.1.refs_1_), custom_call_target="tpu_custom_call" | custom-call | tf_op jit(solution)/shard_map/deposit_more/pallas_call | solution.py:425
  19.5 0.0 collective-permute-done.7.refs_1_
  19.5 5.1 %grid_fields.1 = (f32[4,2,64,128]{3,2,1,0:T(8,128)}, f32[3,4,2,64,128]{4,3,2,1,0:T(8,128)}) custom-call(f32[4,4]{1,0:T(4,128)} %refs_0_.1, f32[8,104,128]{2,1,0:T(8,128)S(1)} %collective-permute-done.7.refs_1_, f32[4,2,80,256]{3,2,1,0:T(8,128)S(1)} %deposit_more.1.refs_2_), custom_call_target="tpu_custom_call" | custom-call | tf_op jit(solution)/shard_map/grid_fields/pallas_call | solution.py:425
  (9 shorter events, 0.1 us)
Async XLA Ops:
  2.9 7.6 %collective-permute-start.2 = (f32[104,128]{1,0:T(8,128)S(1)}, f32[104,128]{1,0:T(8,128)S(1)}, u32[]{:S(2)}, u32[]{:S(2)}) collective-permute-start(f32[104,128]{1,0:T(8,128)S(1)} %sort_beads.1), channel_id=1, source_target_pairs={{0,4},{4,8},{8,12},{12,0},{1,5},{5,9},{9,13},{13,1},{2,6},{6,10},{... | collective-permute-start | bytes 159752 | tf_op jit(solution)/shard_map/ppermute | solution.py:450
  5.9 6.1 %collective-permute-start.1 = (f32[104,128]{1,0:T(8,128)S(1)}, f32[104,128]{1,0:T(8,128)S(1)}, u32[]{:S(2)}, u32[]{:S(2)}) collective-permute-start(f32[104,128]{1,0:T(8,128)S(1)} %sort_beads.1), channel_id=1, source_target_pairs={{0,12},{4,0},{8,4},{12,8},{1,13},{5,1},{9,5},{13,9},{2,14},{6,2},{... | collective-permute-start | bytes 159752 | tf_op jit(solution)/shard_map/ppermute | solution.py:450
  8.0 5.3 %collective-permute-start = (f32[104,128]{1,0:T(8,128)S(1)}, f32[104,128]{1,0:T(8,128)S(1)}, u32[]{:S(2)}, u32[]{:S(2)}) collective-permute-start(f32[104,128]{1,0:T(8,128)S(1)} %sort_beads.1), channel_id=1, source_target_pairs={{0,8},{4,12},{8,0},{12,4},{1,9},{5,13},{9,1},{13,5},{2,10},{6,14},... | collective-permute-start | bytes 159752 | tf_op jit(solution)/shard_map/ppermute | solution.py:450
  9.0 6.0 %collective-permute-start.3 = (f32[1,104,128]{2,1,0:T(8,128)S(1)}, f32[1,104,128]{2,1,0:T(8,128)S(1)}, u32[]{:S(2)}, u32[]{:S(2)}) collective-permute-start(f32[1,104,128]{2,1,0:T(8,128)S(1)} %bitcast.17), channel_id=1, source_target_pairs={{0,2},{2,0},{1,3},{3,1},{4,6},{6,4},{5,7},{7,5},{8,10},{10,8},{9,1... | collective-permute-start | bytes 159752 | tf_op jit(solution)/shard_map/ppermute | solution.py:450
  10.5 7.0 %collective-permute-start.6 = (f32[1,104,128]{2,1,0:T(8,128)S(1)}, f32[1,104,128]{2,1,0:T(8,128)S(1)}, u32[]{:S(2)}, u32[]{:S(2)}) collective-permute-start(f32[1,104,128]{2,1,0:T(8,128)S(1)} %bitcast.18), channel_id=1, source_target_pairs={{0,2},{2,0},{1,3},{3,1},{4,6},{6,4},{5,7},{7,5},{8,10},{10,8},{9,1... | collective-permute-start | bytes 159752 | tf_op jit(solution)/shard_map/ppermute | solution.py:450
  12.1 5.5 %collective-permute-start.5 = (f32[1,104,128]{2,1,0:T(8,128)S(1)}, f32[1,104,128]{2,1,0:T(8,128)S(1)}, u32[]{:S(2)}, u32[]{:S(2)}) collective-permute-start(f32[1,104,128]{2,1,0:T(8,128)S(1)} %bitcast.19), channel_id=1, source_target_pairs={{0,2},{2,0},{1,3},{3,1},{4,6},{6,4},{5,7},{7,5},{8,10},{10,8},{9,1... | collective-permute-start | bytes 159752 | tf_op jit(solution)/shard_map/ppermute | solution.py:450
  13.4 4.1 %collective-permute-start.4 = (f32[1,104,128]{2,1,0:T(8,128)S(1)}, f32[1,104,128]{2,1,0:T(8,128)S(1)}, u32[]{:S(2)}, u32[]{:S(2)}) collective-permute-start(f32[1,104,128]{2,1,0:T(8,128)S(1)} %bitcast.20), channel_id=1, source_target_pairs={{0,2},{2,0},{1,3},{3,1},{4,6},{6,4},{5,7},{7,5},{8,10},{10,8},{9,1... | collective-permute-start | bytes 159752 | tf_op jit(solution)/shard_map/ppermute | solution.py:450
  17.6 1.9 %collective-permute-start.7 = (f32[8,104,128]{2,1,0:T(8,128)S(1)}, f32[8,104,128]{2,1,0:T(8,128)S(1)}, u32[]{:S(2)}, u32[]{:S(2)}) collective-permute-start(f32[8,104,128]{2,1,0:T(8,128)S(1)} %constant_dynamic-update-slice_fusion), channel_id=1, source_target_pairs={{0,1},{1,0},{2,3},{3,2},{4,5},{5,4},{6,7},{7,6},{8,9},{9,8},{10,11... | collective-permute-start | bytes 1277960 | tf_op jit(solution)/shard_map/ppermute | solution.py:450
